TPU v7x, 256 devices: a whole 4x4x8 slice. The times are simulated.
256 devices in a mesh: blk: 128 (over y, z, x_lo, core), bank: 2 (over x_hi).
Axes of the slice: x: 4 (x_hi: 2, x_lo: 2; x = x_hi * 2 + x_lo), y: 4, z: 8, core: 2. Of those that a mesh axis runs over, the one named last changes fastest.
Arguments:
- tile_pool: bfloat16 [512, 256, 256], P('blk'), may hold values from -600 to 600
- tile_list: int32 [256], P('blk'), may hold values from 0 to 3, as said below
- counts: int32 [128], replicated, may hold values from 0 to 2, as said below
- projections: bfloat16 [512, 192, 192], P(('blk', 'bank')), may hold values from -600 to 600
Outputs:
- peak_map: float32 [256, 256, 256], P('blk', 'bank')
- zscore_map: float32 [256, 256, 256], P('blk', 'bank')
Inputs may be any that keep to these rules, and one draw needn't show every extreme that they name: `tile_list`: the 2 entries of one owner are distinct. `counts`: owners 2k and 2k + 1 together hold exactly 2 live slots, and owner 2k holds at least 1 of them.
All inputs are finite; a program needn't handle non-finite values.
Results may differ from a plain program's by a relative error of at most 0.008.
Values may be sent and summed in bfloat16 or wider, within the bound.
A program may use at most 64 MiB of HBM per device.

v0:
```python
import math

import jax
import jax.numpy as jnp
from jax import lax
from jax.sharding import PartitionSpec as P

STEPS = 4


def from_behind(value, axis, steps):
    count = lax.axis_size(axis)
    pairs = [(source, (source + steps) % count) for source in range(count)]
    return lax.ppermute(value, axis, pairs)


def make_tables(edge_len):
    indices = jnp.arange(edge_len, dtype=jnp.int32)
    phase_index = indices[:, None] * indices[None, :] % edge_len
    phase_angle = phase_index.astype(jnp.float32) * (2.0 * math.pi / edge_len)
    cosine = jnp.cos(phase_angle).astype(jnp.bfloat16)
    sine = jnp.sin(phase_angle).astype(jnp.bfloat16)
    forward_cols = jnp.concatenate([cosine, -sine], axis=1)
    stack_rows = jnp.concatenate([cosine, sine], axis=0)
    inverse_rows = jnp.concatenate([cosine, -sine], axis=0)
    return (forward_cols, stack_rows, inverse_rows)


def spectrum(fields, tables):
    forward_cols, stack_rows, inverse_rows = tables
    edge_len = fields.shape[-1]
    row_pass = jnp.einsum(
        "bij,jk->bik", fields, forward_cols, preferred_element_type=jnp.float32
    ).astype(jnp.bfloat16)
    products = jnp.einsum("ij,bjk->bik", stack_rows, row_pass, preferred_element_type=jnp.float32)
    real_part = products[:, :edge_len, :edge_len] + products[:, edge_len:, edge_len:]
    imag_part = products[:, :edge_len, edge_len:] - products[:, edge_len:, :edge_len]
    return jnp.concatenate([real_part, imag_part], axis=-1)


def unit_tiles(tiles):
    as_float = tiles.astype(jnp.float32)
    centre = jnp.mean(as_float, axis=(-2, -1), keepdims=True)
    centred = as_float - centre
    mean_square = jnp.mean(centred * centred, axis=(-2, -1), keepdims=True)
    return (centred / jnp.sqrt(mean_square + 1e-05)).astype(jnp.bfloat16)


def unit_projections(images):
    as_float = images.astype(jnp.float32)
    side = images.shape[-1]
    centre = jnp.mean(as_float, axis=(-2, -1), keepdims=True)
    centred = as_float - centre
    mean_square = jnp.mean(centred * centred, axis=(-2, -1), keepdims=True)
    return (centred / (side * jnp.sqrt(mean_square + 1e-05))).astype(jnp.bfloat16)


def padded_spectra(unit_images, edge_len, tables):
    side = unit_images.shape[-1]
    padded = jnp.pad(unit_images, ((0, 0), (0, edge_len - side), (0, edge_len - side)))
    return spectrum(padded, tables).astype(jnp.bfloat16)


def correlate_block(tile_spec, block_spec, tables):
    forward_cols, stack_rows, inverse_rows = tables
    slot_count = tile_spec.shape[0]
    proj_count = block_spec.shape[0]
    edge_len = block_spec.shape[1]
    tile_real = tile_spec[:, None, :, :edge_len].astype(jnp.float32)
    tile_imag = tile_spec[:, None, :, edge_len:].astype(jnp.float32)
    proj_real = block_spec[None, :, :, :edge_len].astype(jnp.float32)
    proj_imag = block_spec[None, :, :, edge_len:].astype(jnp.float32)
    cross_spec = jnp.concatenate(
        [
            tile_real * proj_real + tile_imag * proj_imag,
            tile_imag * proj_real - tile_real * proj_imag,
        ],
        axis=-1,
    ).astype(jnp.bfloat16)
    cross_spec = cross_spec.reshape(slot_count * proj_count, edge_len, 2 * edge_len)
    products = jnp.einsum("ij,bjk->bik", stack_rows, cross_spec, preferred_element_type=jnp.float32)
    inner_pass = jnp.concatenate(
        [
            products[:, :edge_len, :edge_len] - products[:, edge_len:, edge_len:],
            products[:, edge_len:, :edge_len] + products[:, :edge_len, edge_len:],
        ],
        axis=-1,
    ).astype(jnp.bfloat16)
    correlation = jnp.einsum(
        "bij,jk->bik", inner_pass, inverse_rows, preferred_element_type=jnp.float32
    ) * (1.0 / edge_len)
    return correlation.reshape(slot_count, proj_count, edge_len, edge_len)


def fold_block(stats, block_spec, tile_spec, tables, active):
    best_map, total_map, squares = stats
    correlation = correlate_block(tile_spec, block_spec, tables)
    best_map = jnp.where(active, jnp.maximum(best_map, jnp.max(correlation, axis=1)), best_map)
    total_map = total_map + jnp.where(active, jnp.sum(correlation, axis=1), 0.0)
    squares = squares + jnp.where(active, jnp.sum(correlation * correlation, axis=1), 0.0)
    return (best_map, total_map, squares)


def body(tile_pool, tile_list, counts, projections):
    edge_len = tile_pool.shape[-1]
    slot_total = tile_list.shape[0]
    tables = make_tables(edge_len)
    owner_index = lax.axis_index("blk")
    live_count = counts[owner_index]
    chosen = tile_pool[tile_list]
    is_guest = jnp.zeros((slot_total,), bool)
    positions = STEPS
    tile_spec = (spectrum(unit_tiles(chosen), tables) * (1.0 / edge_len)).astype(jnp.bfloat16)
    proj_unit = unit_projections(projections)
    current = padded_spectra(proj_unit, edge_len, tables)
    work_slots = chosen.shape[0]
    stats = (
        jnp.full((work_slots, edge_len, edge_len), -1e30, jnp.float32),
        jnp.zeros((work_slots, edge_len, edge_len), jnp.float32),
        jnp.zeros((work_slots, edge_len, edge_len), jnp.float32),
    )
    for position in range(positions):
        if position + 1 < positions:
            upcoming = from_behind(current, "blk", 1)
        block_spec = current
        if position == 0:
            active = jnp.logical_not(is_guest)
        else:
            active = jnp.ones_like(is_guest)
        stats = fold_block(stats, block_spec, tile_spec, tables, active[:, None, None])
        if position + 1 < positions:
            current = upcoming
    best_map, total_map, squares = stats
    halves = (
        lax.all_to_all(
            best_map[None].astype(jnp.bfloat16), "bank", split_axis=2, concat_axis=0, tiled=True
        ).astype(jnp.float32),
        lax.all_to_all(
            total_map[None].astype(jnp.bfloat16), "bank", split_axis=2, concat_axis=0, tiled=True
        ).astype(jnp.float32),
        lax.all_to_all(
            squares[None].astype(jnp.bfloat16), "bank", split_axis=2, concat_axis=0, tiled=True
        ).astype(jnp.float32),
    )
    best_map = jnp.max(halves[0], axis=0)
    total_map = jnp.sum(halves[1], axis=0)
    squares = jnp.sum(halves[2], axis=0)
    orient_total = STEPS * lax.axis_size("bank") * projections.shape[0]
    mean_map = total_map / orient_total
    spread_map = jnp.maximum(squares / orient_total - mean_map * mean_map, 0.3)
    score = (best_map - mean_map) / jnp.sqrt(spread_map)
    keep_slot = (jnp.arange(slot_total, dtype=jnp.int32) < live_count)[:, None, None]
    peak_out = jnp.where(keep_slot, best_map, 0.0)
    score_out = jnp.where(keep_slot, score, 0.0)
    return (peak_out, score_out)


def solution(mesh):
    in_specs = (P("blk", None, None), P("blk"), P(), P(("blk", "bank"), None, None))
    out_specs = (P("blk", "bank", None), P("blk", "bank", None))
    return jax.shard_map(body, mesh=mesh, in_specs=in_specs, out_specs=out_specs, check_vma=False)
```

profile of v0, /device:TPU:0, one launch (start us, length us, event | category | flops | bytes accessed | tf_op | source)
XLA Modules:
  0.0 92.4 jit_solution(5097693016122218410)
XLA Ops:
  0.6 0.0 copy-start
  0.6 1.1 %sine_convert_fusion = (bf16[256,256]{1,0:T(8,128)(2,1)S(1)}, bf16[256,256]{1,0:T(8,128)(2,1)S(1)}) fusion(), kind=kLoop, calls=%fused_computation.130 | loop fusion | flops 1048576 | bytes 262144 | tf_op jit(solution)/shard_map/convert_element_type | solution.py:22
  1.7 1.0 %fusion.68 = bf16[256,256]{1,0:T(8,128)(2,1)S(1)} fusion(), kind=kLoop, calls=%fused_computation.137 | loop fusion | flops 1179648 | bytes 131072 | tf_op jit(solution)/shard_map/neg | solution.py:23
  2.7 1.1 %convert_reduce_fusion.3 = f32[2]{0:T(128)S(1)} fusion(bf16[2,192,192]{2,1,0:T(8,128)(2,1)} %param.7), kind=kLoop, calls=%fused_computation.98 | loop fusion | flops 147454 | bytes 147464 | tf_op jit(solution)/shard_map/reduce_sum | solution.py:52
  3.8 1.2 %fusion.45 = f32[2]{0:T(128)S(1)} fusion(bf16[2,192,192]{2,1,0:T(8,128)(2,1)} %param.7, f32[2]{0:T(128)S(1)} %broadcast_multiply_fusion), kind=kLoop, calls=%fused_computation.101 | loop fusion | flops 294910 | bytes 147472 | tf_op jit(solution)/shard_map/reduce_sum | solution.py:54
  5.0 1.0 %fusion.46 = bf16[2,192,192]{2,1,0:T(8,128)(2,1)S(1)} fusion(bf16[2,192,192]{2,1,0:T(8,128)(2,1)} %param.7, f32[2]{0:T(128)S(1)} %sqrt_multiply_fusion, f32[2]{0:T(128)S(1)} %broadcast_multiply_fusion), kind=kLoop, calls=%fused_computation.102 | loop fusion | flops 294912 | bytes 294928 | tf_op jit(solution)/shard_map/convert_element_type | solution.py:55
  6.0 0.7 convolution_bitcast_fusion.4
  6.7 0.0 copy-start.6
  6.8 0.0 copy-start.7
  6.8 1.0 %fusion.93 = (f32[2,256,256]{1,2,0:T(8,128)S(1)}, bf16[2,256,256]{1,2,0:T(8,128)(2,1)S(1)}, f32[2,256,256]{1,2,0:T(8,128)}, bf16[2,256,256]{1,2,0:T(8,128)(2,1)S(1)}) fusion(f32[2,512,512]{1,2,0:T(8,128)S(1)} %convolution_bitcast_fusion.4), kind=kLoop, calls=%fused_computation.156 | loop fusion | flops 786432 | bytes 3670016 | tf_op jit(solution)/shard_map/convert_element_type | solution.py:71
  7.8 0.1 collective-permute-start
  7.9 0.0 copy-done.6
  7.9 0.6 gather_fusion
  8.5 0.2 convert_reduce_fusion
  8.7 0.3 fusion.39
  8.9 0.6 dynamic_slice.3
  9.5 2.1 %convolution_bitcast_fusion.5 = f32[2,512,512]{1,2,0:T(8,128)} fusion(bf16[2,256,256]{2,1,0:T(8,128)(2,1)S(1)} %gather_fusion, f32[2]{0:T(128)S(1)} %add_sqrt_fusion, f32[2]{0:T(128)S(1)} %broadcast_multiply_fusion.1, bf16[256,256]{1,0:T(8,128)(2,1)S(1)} %fusion.68, bf16[256,256]{1,0:T(8,128)(2,1)S(1)} %get-tuple-element.57, ...), kind=kOutput, calls=%fused_computation.6 | convolution fusion | flops 404488192 | bytes 2752528 | tf_op jit(solution)/shard_map/ij,bjk->bik/dot_general | solution.py:35
  11.6 10.0 %collective-permute-done = bf16[2,256,512]{1,2,0:T(8,128)(2,1)S(1)} collective-permute-done((bf16[2,256,512]{1,2,0:T(8,128)(2,1)S(1)}, bf16[2,256,512]{1,2,0:T(8,128)(2,1)S(1)}, u32[]{:S(2)}, u32[]{:S(2)}) %collective-permute-start) | collective-permute-done | bytes 524320 | tf_op jit(solution)/shard_map/ppermute | solution.py:14
  21.6 0.0 collective-permute-start.1
  21.6 1.7 %slice_add_fusion.5 = (f32[2,256,256]{1,2,0:T(8,128)S(1)}, f32[2,256,256]{1,2,0:T(8,128)S(1)}) fusion(f32[2,512,512]{1,2,0:T(8,128)} %convolution_bitcast_fusion.5), kind=kLoop, calls=%fused_computation.90 | loop fusion | flops 262144 | bytes 3145728 | tf_op jit(solution)/shard_map/add | solution.py:36
  23.3 0.1 fusion.8
  23.4 0.1 slice_convert_fusion.7
  23.5 11.0 %collective-permute-done.1 = bf16[2,256,512]{1,2,0:T(8,128)(2,1)S(1)} collective-permute-done((bf16[2,256,512]{1,2,0:T(8,128)(2,1)S(1)}, bf16[2,256,512]{1,2,0:T(8,128)(2,1)S(1)}, u32[]{:S(2)}, u32[]{:S(2)}) %collective-permute-start.1) | collective-permute-done | bytes 524320 | tf_op jit(solution)/shard_map/ppermute | solution.py:14
  34.5 0.0 collective-permute-start.2
  34.5 0.7 iota_compare_fusion
  35.1 0.1 slice_convert_fusion.5
  35.2 0.1 slice_convert_fusion.3
  35.3 12.0 %collective-permute-done.2 = bf16[2,256,512]{1,2,0:T(8,128)(2,1)S(1)} collective-permute-done((bf16[2,256,512]{1,2,0:T(8,128)(2,1)S(1)}, bf16[2,256,512]{1,2,0:T(8,128)(2,1)S(1)}, u32[]{:S(2)}, u32[]{:S(2)}) %collective-permute-start.2) | collective-permute-done | bytes 524320 | tf_op jit(solution)/shard_map/ppermute | solution.py:14
  47.3 0.1 slice_convert_fusion.1
  47.4 0.0 copy-done.1
  47.4 1.3 %add_convert_fusion.3 = (bf16[2,2,256,256]{2,3,1,0:T(8,128)(2,1)S(1)}, bf16[2,2,256,256]{2,3,1,0:T(8,128)(2,1)S(1)}, bf16[2,2,256,256]{2,3,1,0:T(8,128)(2,1)S(1)...) fusion(f32[2,256,256]{1,2,0:T(8,128)S(1)} %copy-done.1, ...), kind=kLoop, calls=%fused_computation.78 | loop fusion | flops 8388608 | bytes 9437184 | tf_op jit(solution)/shard_map/convert.28
  48.7 0.7 convolution_bitcast_fusion.3
  49.5 0.3 fusion.7
  49.8 0.7 convolution_bitcast_fusion.2
  50.5 0.3 fusion.5
  50.8 0.7 convolution_bitcast_fusion.1
  51.5 0.3 fusion.3
  51.8 0.7 convolution_bitcast_fusion
  52.6 0.3 fusion.1
  52.8 1.2 %bitcast_reduce_fusion.6 = (f32[2,256,256]{2,1,0:T(8,128)S(1)}, f32[2,256,256]{2,1,0:T(8,128)S(1)}, bf16[2,256,256]{2,1,0:T(8,128)(2,1)}) fusion(bf16[256,256]{1,0:T(8,128)(2,1)S(1)} %get-tuple-element.57, bf16[256,256]{1,0:T(8,128)(2,1)S(1)} %fusion.68, bf16[4,256,256]{1,2,0:T(8,128)(2,1)S(1)} %get-tuple-element.21, ...), kind=kOutput, calls=%fused_computation.68 | convolution fusion | flops 271974400 | bytes 2621440 | tf_op jit(solution)/shard_map/bij,jk->bik/dot_general | solution.py:89
  54.1 1.2 %bitcast_reduce_fusion.4 = (f32[2,256,256]{2,1,0:T(8,128)S(1)}, f32[2,256,256]{2,1,0:T(8,128)S(1)}, bf16[2,256,256]{2,1,0:T(8,128)(2,1)}) fusion(bf16[256,256]{1,0:T(8,128)(2,1)S(1)} %get-tuple-element.57, bf16[256,256]{1,0:T(8,128)(2,1)S(1)} %fusion.68, bf16[4,256,256]{1,2,0:T(8,128)(2,1)S(1)} %get-tuple-element.23, ...), kind=kOutput, calls=%fused_computation.64 | convolution fusion | flops 271974400 | bytes 2621440 | tf_op jit(solution)/shard_map/bij,jk->bik/dot_general | solution.py:89
  55.3 1.2 %bitcast_reduce_fusion.2 = (f32[2,256,256]{2,1,0:T(8,128)S(1)}, f32[2,256,256]{2,1,0:T(8,128)S(1)}, bf16[2,256,256]{2,1,0:T(8,128)(2,1)}) fusion(bf16[256,256]{1,0:T(8,128)(2,1)S(1)} %get-tuple-element.57, bf16[256,256]{1,0:T(8,128)(2,1)S(1)} %fusion.68, bf16[4,256,256]{1,2,0:T(8,128)(2,1)S(1)} %get-tuple-element.25, ...), kind=kOutput, calls=%fused_computation.60 | convolution fusion | flops 271974400 | bytes 2621440 | tf_op jit(solution)/shard_map/bij,jk->bik/dot_general | solution.py:89
  56.5 1.4 %bitcast_reduce_fusion = (f32[2,256,256]{2,1,0:T(8,128)S(1)}, f32[2,256,256]{2,1,0:T(8,128)}, bf16[2,256,256]{2,1,0:T(8,128)(2,1)}) fusion(bf16[256,256]{1,0:T(8,128)(2,1)S(1)} %get-tuple-element.57, bf16[256,256]{1,0:T(8,128)(2,1)S(1)} %fusion.68, bf16[4,256,256]{1,2,0:T(8,128)(2,1)S(1)} %get-tuple-element.27, bf16[4,256,256]{1,2,0:T(8,128)(2,1)S(1)} %get-tuple-element.26), kind=kOutput, calls=%fused_computation.56 | convolution fusion | flops 271974400 | bytes 2621440 | tf_op jit(solution)/shard_map/bij,jk->bik/dot_general | solution.py:89
  57.9 0.1 fusion.57
  58.0 0.0 copy-start.4
  58.0 0.0 copy-start.5
  58.1 1.0 %copy.21 = bf16[1,2,256,256]{3,1,0,2:T(2,128)(2,1)} copy(bf16[1,2,256,256]{3,2,1,0:T(8,128)(2,1)S(1)} %fusion.57) | data formatting | bytes 524288 | tf_op jit(solution)/shard_map/convert_element_type | solution.py:139
  59.1 4.0 %all-to-all-start.1 = ((bf16[1,2,256,256]{3,1,0,2:T(2,128)(2,1)}), bf16[1,2,256,256]{3,1,0,2:T(2,128)(2,1)S(1)}, u32[]{:S(2)}, u32[]{:S(2)}) async-start(bf16[1,2,256,256]{3,1,0,2:T(2,128)(2,1)} %copy.21), calls=%async_computation.1 | async-start | bytes 524288 | tf_op jit(solution)/shard_map/all_to_all | solution.py:138
  63.0 1.1 %fusion.58 = bf16[1,2,256,256]{3,2,1,0:T(8,128)(2,1)S(1)} fusion(f32[2,256,256]{2,1,0:T(8,128)} %get-tuple-element.14, f32[2,256,256]{2,1,0:T(8,128)S(1)} %get-tuple-element.11, f32[2,256,256]{2,1,0:T(8,128)S(1)} %get-tuple-element.8, f32[2,256,256]{2,1,0:T(8,128)S(1)} %get-tuple-element.5), kind=kLoop, calls=%fused_computation.119 | loop fusion | flops 524288 | bytes 2359296 | tf_op jit(solution)/shard_map/convert_element_type | solution.py:142
  64.2 1.0 %copy.22 = bf16[1,2,256,256]{3,1,0,2:T(2,128)(2,1)} copy(bf16[1,2,256,256]{3,2,1,0:T(8,128)(2,1)S(1)} %fusion.58) | data formatting | bytes 524288 | tf_op jit(solution)/shard_map/convert_element_type | solution.py:142
  65.2 0.0 copy-done.3
  65.2 0.2 fusion.56
  65.3 1.0 %copy.20 = bf16[1,2,256,256]{3,1,0,2:T(2,128)(2,1)} copy(bf16[1,2,256,256]{3,2,1,0:T(8,128)(2,1)S(1)} %fusion.56) | data formatting | bytes 524288 | tf_op jit(solution)/shard_map/max | solution.py:98
  66.3 3.4 %all-to-all-done.1 = bf16[1,2,256,256]{3,1,0,2:T(2,128)(2,1)S(1)} async-done(((bf16[1,2,256,256]{3,1,0,2:T(2,128)(2,1)}), bf16[1,2,256,256]{3,1,0,2:T(2,128)(2,1)S(1)}, u32[]{:S(2)}, u32[]{:S(2)}) %all-to-all-start.1) | async-done | bytes 262176 | tf_op jit(solution)/shard_map/all_to_all | solution.py:138
  69.7 3.4 %all-to-all-start.2 = ((bf16[1,2,256,256]{3,1,0,2:T(2,128)(2,1)}), bf16[1,2,256,256]{3,1,0,2:T(2,128)(2,1)S(1)}, u32[]{:S(2)}, u32[]{:S(2)}) async-start(bf16[1,2,256,256]{3,1,0,2:T(2,128)(2,1)} %copy.22), calls=%async_computation.2 | async-start | bytes 524288 | tf_op jit(solution)/shard_map/all_to_all | solution.py:141
  73.2 0.3 convert_reduce_fusion.2
  73.5 6.4 %all-to-all-done.2 = bf16[1,2,256,256]{3,1,0,2:T(2,128)(2,1)S(1)} async-done(((bf16[1,2,256,256]{3,1,0,2:T(2,128)(2,1)}), bf16[1,2,256,256]{3,1,0,2:T(2,128)(2,1)S(1)}, u32[]{:S(2)}, u32[]{:S(2)}) %all-to-all-start.2) | async-done | bytes 262176 | tf_op jit(solution)/shard_map/all_to_all | solution.py:141
  79.8 3.4 %all-to-all-start = ((bf16[1,2,256,256]{3,1,0,2:T(2,128)(2,1)}), bf16[1,2,256,256]{3,1,0,2:T(2,128)(2,1)S(1)}, u32[]{:S(2)}, u32[]{:S(2)}) async-start(bf16[1,2,256,256]{3,1,0,2:T(2,128)(2,1)} %copy.20), calls=%async_computation | async-start | bytes 524288 | tf_op jit(solution)/shard_map/all_to_all | solution.py:135
  83.3 0.3 convert_reduce_fusion.1
  83.6 6.4 %all-to-all-done = bf16[1,2,256,256]{3,1,0,2:T(2,128)(2,1)S(1)} async-done(((bf16[1,2,256,256]{3,1,0,2:T(2,128)(2,1)}), bf16[1,2,256,256]{3,1,0,2:T(2,128)(2,1)S(1)}, u32[]{:S(2)}, u32[]{:S(2)}) %all-to-all-start) | async-done | bytes 262176 | tf_op jit(solution)/shard_map/all_to_all | solution.py:135
  90.0 0.5 reduce_max.54
  90.5 0.4 fusion.52
  90.9 0.7 copy.23
  91.6 0.7 copy.24
  (15 shorter events, 0.1 us)
Async XLA Ops:
  0.6 7.3 %copy-start = (bf16[4,256,256]{2,1,0:T(8,128)(2,1)S(1)}, bf16[4,256,256]{2,1,0:T(8,128)(2,1)}, u32[]{:S(2)}) copy-start(bf16[4,256,256]{2,1,0:T(8,128)(2,1)} %param.4) | copy-start | bytes 1572868
  6.7 1.1 %copy-start.6 = (s32[2]{0:T(128)S(1)}, s32[2]{0:T(128)}, u32[]{:S(2)}) copy-start(s32[2]{0:T(128)} %param.5) | copy-start | bytes 28
  6.8 2.2 %copy-start.7 = (s32[128]{0:T(128)S(1)}, s32[128]{0:T(128)}, u32[]{:S(2)}) copy-start(s32[128]{0:T(128)} %param.6) | copy-start | bytes 1540
  7.8 13.9 %collective-permute-start = (bf16[2,256,512]{1,2,0:T(8,128)(2,1)S(1)}, bf16[2,256,512]{1,2,0:T(8,128)(2,1)S(1)}, u32[]{:S(2)}, u32[]{:S(2)}) collective-permute-start(bf16[2,256,512]{1,2,0:T(8,128)(2,1)S(1)} %pad_maximum_fusion), channel_id=1, source_target_pairs={{0,2},{2,4},{4,6},{6,8},{8,10},{10,12},{12,14},{14,16},{16,18},{18... | collective-permute-start | bytes 1572872 | tf_op jit(solution)/shard_map/ppermute | solution.py:14
  21.6 12.8 %collective-permute-start.1 = (bf16[2,256,512]{1,2,0:T(8,128)(2,1)S(1)}, bf16[2,256,512]{1,2,0:T(8,128)(2,1)S(1)}, u32[]{:S(2)}, u32[]{:S(2)}) collective-permute-start(bf16[2,256,512]{1,2,0:T(8,128)(2,1)S(1)} %collective-permute-done), channel_id=1, source_target_pairs={{0,2},{2,4},{4,6},{6,8},{8,10},{10,12},{12,14},{14,16},{16,18},{18... | collective-permute-start | bytes 1572872 | tf_op jit(solution)/shard_map/ppermute | solution.py:14
  34.5 12.8 %collective-permute-start.2 = (bf16[2,256,512]{1,2,0:T(8,128)(2,1)S(1)}, bf16[2,256,512]{1,2,0:T(8,128)(2,1)S(1)}, u32[]{:S(2)}, u32[]{:S(2)}) collective-permute-start(bf16[2,256,512]{1,2,0:T(8,128)(2,1)S(1)} %collective-permute-done.1), channel_id=1, source_target_pairs={{0,2},{2,4},{4,6},{6,8},{8,10},{10,12},{12,14},{14,16},{16,18},{18... | collective-permute-start | bytes 1572872 | tf_op jit(solution)/shard_map/ppermute | solution.py:14
  35.1 12.3 %copy-start.1 = (f32[2,256,256]{1,2,0:T(8,128)S(1)}, f32[2,256,256]{1,2,0:T(8,128)}, u32[]{:S(2)}) copy-start(f32[2,256,256]{1,2,0:T(8,128)} %get-tuple-element.38) | copy-start | bytes 1572868
  58.0 7.1 %copy-start.2 = (bf16[2,256,256]{2,1,0:T(8,128)(2,1)S(1)}, bf16[2,256,256]{2,1,0:T(8,128)(2,1)}, u32[]{:S(2)}) copy-start(bf16[2,256,256]{2,1,0:T(8,128)(2,1)} %get-tuple-element.9) | copy-start | bytes 786436
  58.0 7.1 %copy-start.3 = (bf16[2,256,256]{2,1,0:T(8,128)(2,1)S(1)}, bf16[2,256,256]{2,1,0:T(8,128)(2,1)}, u32[]{:S(2)}) copy-start(bf16[2,256,256]{2,1,0:T(8,128)(2,1)} %get-tuple-element.6) | copy-start | bytes 786436
  58.0 7.1 %copy-start.4 = (bf16[2,256,256]{2,1,0:T(8,128)(2,1)S(1)}, bf16[2,256,256]{2,1,0:T(8,128)(2,1)}, u32[]{:S(2)}) copy-start(bf16[2,256,256]{2,1,0:T(8,128)(2,1)} %get-tuple-element.12) | copy-start | bytes 786436
  58.0 7.1 %copy-start.5 = (bf16[2,256,256]{2,1,0:T(8,128)(2,1)S(1)}, bf16[2,256,256]{2,1,0:T(8,128)(2,1)}, u32[]{:S(2)}) copy-start(bf16[2,256,256]{2,1,0:T(8,128)(2,1)} %get-tuple-element.15) | copy-start | bytes 786436
  59.1 10.7 %all-to-all-start.1 = ((bf16[1,2,256,256]{3,1,0,2:T(2,128)(2,1)}), bf16[1,2,256,256]{3,1,0,2:T(2,128)(2,1)S(1)}, u32[]{:S(2)}, u32[]{:S(2)}) async-start(bf16[1,2,256,256]{3,1,0,2:T(2,128)(2,1)} %copy.21), calls=%async_computation.1 | async-start | bytes 524288 | tf_op jit(solution)/shard_map/all_to_all | solution.py:138
  69.7 10.1 %all-to-all-start.2 = ((bf16[1,2,256,256]{3,1,0,2:T(2,128)(2,1)}), bf16[1,2,256,256]{3,1,0,2:T(2,128)(2,1)S(1)}, u32[]{:S(2)}, u32[]{:S(2)}) async-start(bf16[1,2,256,256]{3,1,0,2:T(2,128)(2,1)} %copy.22), calls=%async_computation.2 | async-start | bytes 524288 | tf_op jit(solution)/shard_map/all_to_all | solution.py:141
  79.8 10.1 %all-to-all-start = ((bf16[1,2,256,256]{3,1,0,2:T(2,128)(2,1)}), bf16[1,2,256,256]{3,1,0,2:T(2,128)(2,1)S(1)}, u32[]{:S(2)}, u32[]{:S(2)}) async-start(bf16[1,2,256,256]{3,1,0,2:T(2,128)(2,1)} %copy.20), calls=%async_computation | async-start | bytes 524288 | tf_op jit(solution)/shard_map/all_to_all | solution.py:135
where the time goes:
time: 92.8 us; the launch traced here: 92.4 us
  waiting for transfers between devices  49.1 us (53%)
  other arithmetic  15 us (16%)
  starting transfers between devices  11 us (12%)
  matrix products  10.8 us (12%)
  local copies, waits for them, and re-layouts  5.56 us (6%)
  between operations  0.93 us (1%)
    ppermute x3, waiting for transfers between devices, from_behind(): return lax.ppermute(value, axis, pairs)  33 us
    all_to_all x1, waiting for transfers between devices, body(): lax.all_to_all(squares[None].astype(jnp.bfloat16), 'bank', split_axis=2,...  6.37 us
    all_to_all x1, waiting for transfers between devices, body(): lax.all_to_all(best_map[None].astype(jnp.bfloat16), 'bank', split_axis=2,...  6.37 us
    dot_general x4, matrix products, correlate_block(): jnp.einsum('bij,jk->bik', inner_pass, inverse_rows, preferred_element_typ...  5.03 us
    all_to_all x1, starting transfers between devices, body(): lax.all_to_all(total_map[None].astype(jnp.bfloat16), 'bank', split_axis=2...  3.99 us
    all_to_all x1, starting transfers between devices, body(): lax.all_to_all(best_map[None].astype(jnp.bfloat16), 'bank', split_axis=2,...  3.44 us
    all_to_all x1, starting transfers between devices, body(): lax.all_to_all(squares[None].astype(jnp.bfloat16), 'bank', split_axis=2,...  3.44 us
    all_to_all x1, waiting for transfers between devices, body(): lax.all_to_all(total_map[None].astype(jnp.bfloat16), 'bank', split_axis=2...  3.42 us
  transfers between devices with their start and end apart: 6, of which 6 were waited for; matrix products, arithmetic and copies ran while one was open for 11% of the time, Pallas kernels for 0%

commit v1 on v0

v1 whole, which is shorter than its diff:
```python
import functools

import jax
import jax.numpy as jnp
import ml_dtypes
import numpy as np
from jax import lax
from jax.experimental import pallas as pl
from jax.experimental.pallas import tpu as pltpu
from jax.sharding import PartitionSpec as P

EDGE = 256
SIDE = 192
HALF = 128
CHIPS = 64
UNIT = (288, 128)
BF16 = jnp.bfloat16
F32 = jnp.float32
MESH = pl.DeviceIdType.MESH
STAGE = 16


def slot(block, bank, r):
    return (block * 2 + bank) * 2 + r


def make_tables():
    index = np.arange(EDGE)
    angle = (index[:, None] * index[None, :] % EDGE) * (2.0 * np.pi / EDGE)
    cosine = np.cos(angle)
    sine = np.sin(angle)
    alternate = 1.0 - 2.0 * (index % 2)
    row_pass = np.concatenate([cosine[:, :HALF], -sine[:, :HALF]], axis=1)
    row_pass[:, HALF] = alternate
    first = np.zeros((EDGE, EDGE))
    first[:SIDE] = row_pass[:SIDE]
    second = np.zeros((EDGE, EDGE))
    second[:HALF] = row_pass[:HALF]
    second[SIDE:] = row_pass[HALF:SIDE]
    rows = np.stack([row_pass, first, second])
    tile_cols = np.block([[cosine, sine], [-sine, cosine]])
    proj_cols = np.block(
        [[cosine[:, :SIDE], sine[:, :SIDE]], [-sine[:, :SIDE], cosine[:, :SIDE]]]
    )
    back_cols = np.stack(
        [
            np.block(
                [
                    [cosine[part : part + HALF], -sine[part : part + HALF]],
                    [sine[part : part + HALF], cosine[part : part + HALF]],
                ]
            )
            for part in (0, HALF)
        ]
    )
    back_rows = np.concatenate([2.0 * cosine[:HALF], -2.0 * sine[:HALF]], axis=0)
    back_rows[0] = 1.0
    back_rows[HALF] = alternate
    back_rows /= EDGE
    cast = lambda table: table.astype(np.float32).astype(ml_dtypes.bfloat16)
    alt_rows = np.broadcast_to(alternate, (16, EDGE))
    flip_rows = np.eye(HALF)[::-1]
    return tuple(cast(t) for t in (rows, tile_cols, proj_cols, back_cols, back_rows, alt_rows, flip_rows))


def dot(a, b):
    return jnp.dot(a, b, preferred_element_type=F32)


def kernel(
    pool, tile_list, counts, raw, rows, tile_cols, proj_cols, back_cols, back_rows, alt_rows, flip_rows,
    peak_out, score_out,
    buf, back, spec_re, spec_im, circ, stats, send_sem, recv_sem, load_sem,
):
    me = lax.axis_index("blk")
    bank = lax.axis_index("bank")
    chip = me // 2
    core = me % 2
    odd = chip % 2
    other = 1 - bank

    def device(ahead, which, side):
        return (((chip + ahead + CHIPS) % CHIPS) * 2 + which, side)

    load = pltpu.make_async_copy(back_cols.at[bank], back, load_sem)
    load.start()
    barrier = pltpu.get_barrier_semaphore()

    def greet(target):
        pl.semaphore_signal(barrier, inc=1, device_id=target, device_id_type=MESH)

    greet(device(0, 1 - core, bank))
    greet(device(0, 0, other))

    @pl.when(core == 1)
    def _():
        greet(device(0, 1, other))

    @pl.when(odd == 0)
    def _():
        greet(device(1, core, bank))
        greet(device(1, core, other))

        @pl.when(core == 0)
        def _():
            greet(device(-2, 1, bank))

    @pl.when(odd == 1)
    def _():
        for side in (bank, other):
            for which in (0, 1):
                greet(device(-1, which, side))
        for which in (0, 1):
            greet(device(-2, which, bank))

    for r in range(2):
        image = raw[r].astype(F32)
        centred = image - jnp.sum(image) * (1.0 / (SIDE * SIDE))
        power = jnp.sum(centred * centred) * (1.0 / (SIDE * SIDE))
        unit = centred / (SIDE * jnp.sqrt(power + 1e-5))
        right = jnp.concatenate([unit[:96, HALF:], unit[96:, HALF:]], axis=1)
        packed = jnp.concatenate([unit[:, :HALF], right], axis=0).astype(BF16)

        @pl.when(core == 0)
        def _():
            buf[slot(0, 0, r)] = packed

        @pl.when(core == 1)
        def _():
            buf[slot(1, 0, r)] = packed

    @pl.when((odd == 1) & (core == 1))
    def _():
        pl.semaphore_wait(barrier, 6)

    @pl.when((odd == 0) | (core == 0))
    def _():
        pl.semaphore_wait(barrier, 7)

    def gather(core, odd):
        sends = []

        def send(source, target, to):
            copy = pltpu.make_async_remote_copy(
                src_ref=buf.at[source],
                dst_ref=buf.at[target],
                send_sem=send_sem.at[len(sends)],
                recv_sem=recv_sem.at[target],
                device_id=to,
                device_id_type=MESH,
            )
            copy.start()
            sends.append(copy)

        def arrive(target):
            pltpu.make_async_remote_copy(
                src_ref=buf.at[target],
                dst_ref=buf.at[target],
                send_sem=send_sem.at[0],
                recv_sem=recv_sem.at[target],
                device_id=device(0, 1 - core, bank),
                device_id_type=MESH,
            ).wait_recv()

        def share(at):
            send(at, at, device(0, 1 - core, bank))

        own = [slot(core, 0, r) for r in range(2)]
        sides = ((0, bank), (1, other))
        if odd:
            for r in range(2):
                target = slot(1, 0, 0) if core == 1 and r == 0 else STAGE + 1 - core
                send(own[r], target, device(2, r, bank))
        elif core == 1:
            for r in range(2):
                send(own[r], slot(1, 0, r), device(2, 0, bank))
        for r in range(2):
            send(own[r], slot(core, 1, r), device(0, 1 if core == 1 else r, other))
        if not odd:
            for r in range(2):
                for at, side in sides:
                    send(own[r], slot(2 + core, at, r), device(1, r, side))
        if core == 0:
            for r in range(2):
                send(own[r], own[r], device(0, 1, bank))
        if odd:
            for which in (1, 0):
                at = slot(1, 0, 0) if which == 1 and core == 0 else STAGE + 1 - which
                arrive(at)
                for to, side in sides:
                    send(at, slot(2 + which, to, core), device(-1, core, side))
                if which == 1 and core == 1:
                    send(at, slot(1, 0, 1), device(0, 0, bank))
        if core == 1:
            for r in range(2):
                arrive(slot(1, 1, r))
                send(slot(1, 1, r), slot(1, 1, r), device(2, 0, bank))
        arrive(slot(0, 1, core))
        share(slot(0, 1, core))
        for block in (3, 2):
            for at in range(2):
                arrive(slot(block, at, core))
                share(slot(block, at, core))
        if core == 1:
            for r in range(2):
                arrive(slot(0, 0, r))
        arrive(slot(0, 1, 1 - core))
        for block in (3, 2):
            for at in range(2):
                arrive(slot(block, at, 1 - core))
        if core == 0:
            for r in range(2):
                if not (odd and r == 0):
                    arrive(slot(1, 0, r))
            for r in range(2):
                arrive(slot(1, 1, r))
        for copy in sends:
            copy.wait_send()

    for which in (0, 1):
        for parity in (0, 1):
            pl.when((core == which) & (odd == parity))(functools.partial(gather, which, parity))

    lane = lax.broadcasted_iota(jnp.int32, (1, EDGE), 1)
    is_edge = (lane % HALF) == 0

    res, ims = [], []
    for s in range(2):
        image = pool[tile_list[s]].astype(F32)
        centred = image - jnp.sum(image) * (1.0 / (EDGE * EDGE))
        power = jnp.sum(centred * centred) * (1.0 / (EDGE * EDGE))
        unit = (centred / jnp.sqrt(power + 1e-5)).astype(BF16)
        passed = dot(unit, rows[0])
        res.append(passed[:, :HALF])
        ims.append(passed[:, HALF:])
        column = lax.dot_general(
            alt_rows[...], unit, (((1,), (1,)), ((), ())), preferred_element_type=F32
        )
        column = column[:8]
        swapped = jnp.concatenate([column[:, HALF:], column[:, :HALF]], axis=1)
        column = jnp.where(bank == 1, swapped, column)
        spread = jnp.broadcast_to(column[:1], (HALF, EDGE))
        spread = pltpu.roll(spread, HALF + 1, 1, stride=1, stride_axis=0)
        circ[s] = dot(flip_rows[...], spread[:, :SIDE].astype(BF16)).astype(BF16)
    tile_re = jnp.concatenate(res, axis=1).astype(BF16)
    tile_im = jnp.where(is_edge, 0.0, jnp.concatenate(ims, axis=1)).astype(BF16)
    products = dot(tile_cols[...], jnp.concatenate([tile_re, tile_im], axis=0)) * (1.0 / EDGE)
    for s in range(2):
        part = products[:, s * HALF : (s + 1) * HALF].astype(BF16).astype(F32)
        double = jnp.concatenate([part, part], axis=1)
        spec_re[s] = double[:EDGE]
        spec_im[s] = double[EDGE:]

    stats[:, 0] = jnp.full((2, HALF, EDGE), -1e30, F32)
    stats[:, 1:] = jnp.zeros((2, 2, HALF, EDGE), F32)

    def block_step(block, carry):
        parts_re, parts_im = [], []
        for r in range(2):
            unit = buf[block * 2 + r]
            right = unit[SIDE:]
            top = dot(jnp.concatenate([unit[:96], right], axis=1), rows[1])
            bottom = dot(jnp.concatenate([unit[96:SIDE], right], axis=1), rows[2])
            passed = jnp.concatenate([top, bottom], axis=0)
            parts_re.append(passed[:, :HALF])
            parts_im.append(passed[:, HALF:])
        row_re = jnp.concatenate(parts_re, axis=1).astype(BF16)
        row_im = jnp.concatenate(parts_im, axis=1)
        row_edge = jnp.where(is_edge, row_im, 0.0).astype(BF16)
        row_im = jnp.where(is_edge, 0.0, row_im).astype(BF16)
        products = dot(proj_cols[...], jnp.concatenate([row_re, row_im], axis=0))
        proj_re = products[:EDGE].astype(BF16).astype(F32)
        proj_im = products[EDGE:].astype(BF16).astype(F32)
        for s in range(2):
            cross_re = spec_re[s] * proj_re + spec_im[s] * proj_im
            cross_im = spec_im[s] * proj_re - spec_re[s] * proj_im
            cross = jnp.concatenate([cross_re.astype(BF16), cross_im.astype(BF16)], axis=0)
            inner = dot(back[...], cross)
            inner_re = inner[:HALF].astype(BF16)
            inner_im = (inner[HALF:] + dot(circ[s], row_edge)).astype(BF16)
            stacked = jnp.concatenate(
                [
                    jnp.concatenate([inner_re[:, :HALF], inner_im[:, :HALF]], axis=1),
                    jnp.concatenate([inner_re[:, HALF:], inner_im[:, HALF:]], axis=1),
                ],
                axis=0,
            )
            corr = dot(stacked, back_rows[...])
            one, two = corr[:HALF], corr[HALF:]
            stats[s, 0] = jnp.maximum(stats[s, 0], jnp.maximum(one, two))
            stats[s, 1] = stats[s, 1] + (one + two)
            stats[s, 2] = stats[s, 2] + (one * one + two * two)
        return carry

    load.wait()
    lax.fori_loop(0, 8, block_step, 0)

    live = counts[me]
    for s in range(2):
        keep = s < live
        peak = stats[s, 0]
        mean = stats[s, 1] * (1.0 / 16)
        variance = jnp.maximum(stats[s, 2] * (1.0 / 16) - mean * mean, 0.3)
        peak_out[s] = jnp.where(keep, peak, 0.0)
        score_out[s] = jnp.where(keep, (peak - mean) / jnp.sqrt(variance), 0.0)


def body(tile_pool, tile_list, counts, projections):
    tables = make_tables()
    rows, tile_cols, proj_cols, back_cols, back_rows, alt_rows, flip_rows = [jnp.asarray(t) for t in tables]
    vmem = pl.BlockSpec(memory_space=pltpu.VMEM)
    smem = pl.BlockSpec(memory_space=pltpu.SMEM)
    out = jax.ShapeDtypeStruct((2, HALF, EDGE), F32)
    return pl.pallas_call(
        kernel,
        out_shape=(out, out),
        in_specs=[vmem, smem, smem] + [vmem] * 4
        + [pl.BlockSpec(memory_space=pl.ANY), vmem, vmem, vmem],
        out_specs=(vmem, vmem),
        scratch_shapes=[
            pltpu.VMEM((STAGE + 2,) + UNIT, BF16),
            pltpu.VMEM((EDGE, 2 * EDGE), BF16),
            pltpu.VMEM((2, EDGE, EDGE), F32),
            pltpu.VMEM((2, EDGE, EDGE), F32),
            pltpu.VMEM((2, HALF, SIDE), BF16),
            pltpu.VMEM((2, 3, HALF, EDGE), F32),
            pltpu.SemaphoreType.DMA((24,)),
            pltpu.SemaphoreType.DMA((STAGE + 2,)),
            pltpu.SemaphoreType.DMA,
        ],
        compiler_params=pltpu.CompilerParams(
            collective_id=0, has_side_effects=True, vmem_limit_bytes=48 << 20
        ),
    )(tile_pool, tile_list, counts, projections, rows, tile_cols, proj_cols, back_cols, back_rows, alt_rows, flip_rows)


def solution(mesh):
    in_specs = (P("blk", None, None), P("blk"), P(), P(("blk", "bank"), None, None))
    out_specs = (P("blk", "bank", None), P("blk", "bank", None))
    return jax.shard_map(body, mesh=mesh, in_specs=in_specs, out_specs=out_specs, check_vma=False)
```

time: 92.8 us -> 47.1 us (0.51)
  the two profiles are of different devices: /device:TPU:0 before, /device:TPU:1 now
where the time goes in v1:
time: 47.1 us; the launch traced here: 46.6 us
  Pallas kernels  34.9 us (74%)
  local copies, waits for them, and re-layouts  11.1 us (24%)
  between operations  0.66 us (1%)
    pallas_call x1, Pallas kernels, body(): pl.pallas_call(kernel, out_shape=(out, out), in_specs=[vmem, smem, smem]...  34.9 us
    unnamed x24, local copies, waits for them, and re-layouts  11.1 us

profile of v1, /device:TPU:1, one launch (start us, length us, event | category | flops | bytes accessed | tf_op | source)
XLA Modules:
  0.0 46.6 jit_solution(13175350698398405372)
XLA Ops:
  0.6 0.0 copy-start.8
  0.6 0.7 %copy-done.8 = bf16[16,256]{1,0:T(8,128)(2,1)S(1)} copy-done((bf16[16,256]{1,0:T(8,128)(2,1)S(1)}, bf16[16,256]{1,0:T(8,128)(2,1)}, u32[]{:S(2)}) %copy-start.8) | copy-done | bytes 8216
  1.3 0.0 copy-start
  1.3 1.0 %copy-done = bf16[4,256,256]{2,1,0:T(8,128)(2,1)S(1)} copy-done((bf16[4,256,256]{2,1,0:T(8,128)(2,1)S(1)}, bf16[4,256,256]{2,1,0:T(8,128)(2,1)}, u32[]{:S(2)}) %copy-start) | copy-done | bytes 524312
  2.4 0.0 copy-start.1
  2.4 1.0 %copy-done.1 = bf16[2,256,512]{2,1,0:T(8,128)(2,1)S(1)} copy-done((bf16[2,256,512]{2,1,0:T(8,128)(2,1)S(1)}, bf16[2,256,512]{2,1,0:T(8,128)(2,1)}, u32[]{:S(2)}) %copy-start.1) | copy-done | bytes 524312
  3.4 0.0 copy-start.2
  3.4 1.0 %copy-done.2 = bf16[512,512]{1,0:T(8,128)(2,1)S(1)} copy-done((bf16[512,512]{1,0:T(8,128)(2,1)S(1)}, bf16[512,512]{1,0:T(8,128)(2,1)}, u32[]{:S(2)}) %copy-start.2) | copy-done | bytes 524312
  4.5 0.0 copy-start.3
  4.5 1.0 %copy-done.3 = bf16[512,384]{1,0:T(8,128)(2,1)S(1)} copy-done((bf16[512,384]{1,0:T(8,128)(2,1)S(1)}, bf16[512,384]{1,0:T(8,128)(2,1)}, u32[]{:S(2)}) %copy-start.3) | copy-done | bytes 393240
  5.5 0.0 copy-start.4
  5.5 1.0 %copy-done.4 = bf16[3,256,256]{2,1,0:T(8,128)(2,1)S(1)} copy-done((bf16[3,256,256]{2,1,0:T(8,128)(2,1)S(1)}, bf16[3,256,256]{2,1,0:T(8,128)(2,1)}, u32[]{:S(2)}) %copy-start.4) | copy-done | bytes 393240
  6.5 0.0 copy-start.5
  6.5 0.9 %copy-done.5 = bf16[2,192,192]{2,1,0:T(8,128)(2,1)S(1)} copy-done((bf16[2,192,192]{2,1,0:T(8,128)(2,1)S(1)}, bf16[2,192,192]{2,1,0:T(8,128)(2,1)}, u32[]{:S(2)}) %copy-start.5) | copy-done | bytes 147480
  7.4 0.0 copy-start.6
  7.4 0.9 %copy-done.6 = bf16[256,256]{1,0:T(8,128)(2,1)S(1)} copy-done((bf16[256,256]{1,0:T(8,128)(2,1)S(1)}, bf16[256,256]{1,0:T(8,128)(2,1)}, u32[]{:S(2)}) %copy-start.6) | copy-done | bytes 131096
  8.3 0.0 copy-start.7
  8.3 0.8 %copy-done.7 = bf16[128,128]{1,0:T(8,128)(2,1)S(1)} copy-done((bf16[128,128]{1,0:T(8,128)(2,1)S(1)}, bf16[128,128]{1,0:T(8,128)(2,1)}, u32[]{:S(2)}) %copy-start.7) | copy-done | bytes 32792
  9.0 0.0 copy-start.9
  9.0 0.7 %copy-done.9 = s32[2]{0:T(128)S(1)} copy-done((s32[2]{0:T(128)S(1)}, s32[2]{0:T(128)}, u32[]{:S(2)}) %copy-start.9) | copy-done | bytes 32
  9.7 0.0 copy-start.10
  9.7 0.7 %copy-done.10 = s32[128]{0:T(128)S(1)} copy-done((s32[128]{0:T(128)S(1)}, s32[128]{0:T(128)}, u32[]{:S(2)}) %copy-start.10) | copy-done | bytes 536
  10.4 34.9 %shard_map.122 = (f32[2,128,256]{2,1,0:T(8,128)S(1)}, f32[2,128,256]{2,1,0:T(8,128)S(1)}) custom-call(bf16[4,256,256]{2,1,0:T(8,128)(2,1)S(1)} %copy-done, s32[2]{0:T(128)S(1)} %copy-done.9, s32[128]{0:T(128)S(1)} %copy-done.10, bf16[2,192,192]{2,1,0:T(8,128)(2,1)S(1)} %copy-done.5, bf16[3,256,256]{2,1,0:T(8,128)(2,1)S(1)} %copy-done.4, ...), custom_call_target="tpu_custom_call" | custom-call | tf_op jit(solution)/shard_map/pallas_call | solution.py:314
  45.2 0.7 %copy.15 = f32[2,128,256]{2,1,0:T(8,128)} copy(f32[2,128,256]{2,1,0:T(8,128)S(1)} %get-tuple-element.4) | data formatting | bytes 524288
  45.9 0.7 %copy.16 = f32[2,128,256]{2,1,0:T(8,128)} copy(f32[2,128,256]{2,1,0:T(8,128)S(1)} %get-tuple-element.5) | data formatting | bytes 524288
Async XLA Ops:
  0.6 0.7 %copy-start.8 = (bf16[16,256]{1,0:T(8,128)(2,1)S(1)}, bf16[16,256]{1,0:T(8,128)(2,1)}, u32[]{:S(2)}) copy-start(bf16[16,256]{1,0:T(8,128)(2,1)} %constant.19.clone.alt_rows) | copy-start | bytes 24580
  1.3 1.0 %copy-start = (bf16[4,256,256]{2,1,0:T(8,128)(2,1)S(1)}, bf16[4,256,256]{2,1,0:T(8,128)(2,1)}, u32[]{:S(2)}) copy-start(bf16[4,256,256]{2,1,0:T(8,128)(2,1)} %pool.1) | copy-start | bytes 1572868
  2.4 1.0 %copy-start.1 = (bf16[2,256,512]{2,1,0:T(8,128)(2,1)S(1)}, bf16[2,256,512]{2,1,0:T(8,128)(2,1)}, u32[]{:S(2)}) copy-start(bf16[2,256,512]{2,1,0:T(8,128)(2,1)} %constant.17.clone.back_cols) | copy-start | bytes 1572868
  3.4 1.0 %copy-start.2 = (bf16[512,512]{1,0:T(8,128)(2,1)S(1)}, bf16[512,512]{1,0:T(8,128)(2,1)}, u32[]{:S(2)}) copy-start(bf16[512,512]{1,0:T(8,128)(2,1)} %constant.15.clone.tile_cols) | copy-start | bytes 1572868
  4.5 1.0 %copy-start.3 = (bf16[512,384]{1,0:T(8,128)(2,1)S(1)}, bf16[512,384]{1,0:T(8,128)(2,1)}, u32[]{:S(2)}) copy-start(bf16[512,384]{1,0:T(8,128)(2,1)} %constant.16.clone.proj_cols) | copy-start | bytes 1179652
  5.5 1.0 %copy-start.4 = (bf16[3,256,256]{2,1,0:T(8,128)(2,1)S(1)}, bf16[3,256,256]{2,1,0:T(8,128)(2,1)}, u32[]{:S(2)}) copy-start(bf16[3,256,256]{2,1,0:T(8,128)(2,1)} %constant.14.clone.rows) | copy-start | bytes 1179652
  6.5 0.9 %copy-start.5 = (bf16[2,192,192]{2,1,0:T(8,128)(2,1)S(1)}, bf16[2,192,192]{2,1,0:T(8,128)(2,1)}, u32[]{:S(2)}) copy-start(bf16[2,192,192]{2,1,0:T(8,128)(2,1)} %raw.1) | copy-start | bytes 442372
  7.4 0.9 %copy-start.6 = (bf16[256,256]{1,0:T(8,128)(2,1)S(1)}, bf16[256,256]{1,0:T(8,128)(2,1)}, u32[]{:S(2)}) copy-start(bf16[256,256]{1,0:T(8,128)(2,1)} %constant.18.clone.back_rows) | copy-start | bytes 393220
  8.3 0.8 %copy-start.7 = (bf16[128,128]{1,0:T(8,128)(2,1)S(1)}, bf16[128,128]{1,0:T(8,128)(2,1)}, u32[]{:S(2)}) copy-start(bf16[128,128]{1,0:T(8,128)(2,1)} %constant.20.clone.flip_rows) | copy-start | bytes 98308
  9.0 0.7 %copy-start.9 = (s32[2]{0:T(128)S(1)}, s32[2]{0:T(128)}, u32[]{:S(2)}) copy-start(s32[2]{0:T(128)} %tile_list.1) | copy-start | bytes 28
  9.7 0.7 %copy-start.10 = (s32[128]{0:T(128)S(1)}, s32[128]{0:T(128)}, u32[]{:S(2)}) copy-start(s32[128]{0:T(128)} %counts.1) | copy-start | bytes 1540

commit v2 on v1

v2 whole, which is shorter than its diff:
```python
import functools

import jax
import jax.numpy as jnp
import ml_dtypes
import numpy as np
from jax import lax
from jax.experimental import pallas as pl
from jax.experimental.pallas import tpu as pltpu
from jax.sharding import PartitionSpec as P

EDGE = 256
SIDE = 192
HALF = 128
CHIPS = 64
UNIT = (288, 128)
BF16 = jnp.bfloat16
F32 = jnp.float32
MESH = pl.DeviceIdType.MESH
STAGE = 10


def slot(block, at):
    return block * 2 + at


def make_tables():
    index = np.arange(EDGE)
    angle = (index[:, None] * index[None, :] % EDGE) * (2.0 * np.pi / EDGE)
    cosine = np.cos(angle)
    sine = np.sin(angle)
    alternate = 1.0 - 2.0 * (index % 2)
    row_pass = np.concatenate([cosine[:, :HALF], -sine[:, :HALF]], axis=1)
    row_pass[:, HALF] = alternate
    first = np.zeros((EDGE, EDGE))
    first[:SIDE] = row_pass[:SIDE]
    second = np.zeros((EDGE, EDGE))
    second[:HALF] = row_pass[:HALF]
    second[SIDE:] = row_pass[HALF:SIDE]
    rows = np.stack([row_pass, first, second])
    tile_cols = np.block([[cosine, sine], [-sine, cosine]])
    proj_cols = np.block(
        [[cosine[:, :SIDE], sine[:, :SIDE]], [-sine[:, :SIDE], cosine[:, :SIDE]]]
    )
    back_cols = np.stack(
        [
            np.block(
                [
                    [cosine[part : part + HALF], -sine[part : part + HALF]],
                    [sine[part : part + HALF], cosine[part : part + HALF]],
                ]
            )
            for part in (0, HALF)
        ]
    )
    back_rows = np.concatenate([2.0 * cosine[:HALF], -2.0 * sine[:HALF]], axis=0)
    back_rows[0] = 1.0
    back_rows[HALF] = alternate
    back_rows /= EDGE
    cast = lambda table: table.astype(np.float32).astype(ml_dtypes.bfloat16)
    alt_rows = np.broadcast_to(alternate, (16, EDGE))
    flip_rows = np.eye(HALF)[::-1]
    return tuple(cast(t) for t in (rows, tile_cols, proj_cols, back_cols, back_rows, alt_rows, flip_rows))


def dot(a, b):
    return jnp.dot(a, b, preferred_element_type=F32)


def kernel(
    pool_in, tile_list, counts, raw_in, rows_in, tile_cols_in, proj_cols_in, back_cols_in,
    back_rows_in, alt_in, flip_in,
    peak_out, score_out,
    pool, raw, rows, tile_cols, proj_cols, back, back_rows, alt_rows, flip_rows,
    mine, buf, chosen, landed, spec, circ, stats, parts, taken,
    load_sem, send_sem, recv_sem, tile_send, tile_recv, part_send, part_recv,
):
    me = lax.axis_index("blk")
    bank = lax.axis_index("bank")
    chip = me // 2
    core = me % 2
    odd = chip % 2
    other = 1 - bank

    def device(ahead, which, side):
        return (((chip + ahead + CHIPS) % CHIPS) * 2 + which, side)

    sibling = device(0, 1 - core, bank)
    sources = (
        raw_in, pool_in, rows_in, alt_in, flip_in, tile_cols_in, proj_cols_in,
        back_cols_in.at[bank], back_rows_in,
    )
    targets = (raw, pool, rows, alt_rows, flip_rows, tile_cols, proj_cols, back, back_rows)
    loads = [
        pltpu.make_async_copy(source, target, load_sem.at[n])
        for n, (source, target) in enumerate(zip(sources, targets))
    ]
    for load in loads:
        load.start()

    barrier = pltpu.get_barrier_semaphore()

    def greet(target):
        pl.semaphore_signal(barrier, inc=1, device_id=target, device_id_type=MESH)

    greet(sibling)
    greet(device(0, 0, other))
    greet(device(0, 1, other))
    greet(device(-2, 1, bank))

    @pl.when(odd == 0)
    def _():
        greet(device(1, core, bank))
        greet(device(1, core, other))

    @pl.when((odd == 1) | (core == 0))
    def _():
        greet(device(-2, 0, bank))

    @pl.when(odd == 1)
    def _():
        for side in (bank, other):
            for which in (0, 1):
                greet(device(-1, which, side))

    loads[0].wait()
    for r in range(2):
        image = raw[r].astype(F32)
        centred = image - jnp.sum(image) * (1.0 / (SIDE * SIDE))
        power = jnp.sum(centred * centred) * (1.0 / (SIDE * SIDE))
        unit = centred / (SIDE * jnp.sqrt(power + 1e-5))
        right = jnp.concatenate([unit[:96, HALF:], unit[96:, HALF:]], axis=1)
        packed = jnp.concatenate([unit[:, :HALF], right], axis=0).astype(BF16)
        mine[r] = packed

        @pl.when(core == r)
        def _():
            buf[slot(r, 0)] = packed

    loads[1].wait()
    for s in range(2):
        chosen[s] = pool[tile_list[s]]

    @pl.when(odd == 1)
    def _():
        pl.semaphore_wait(barrier, 7)

    @pl.when((odd == 0) & (core == 0))
    def _():
        pl.semaphore_wait(barrier, 8)

    @pl.when((odd == 0) & (core == 1))
    def _():
        pl.semaphore_wait(barrier, 9)

    variants = [(which, parity) for which in (0, 1) for parity in (0, 1)]
    sent = {variant: 0 for variant in variants}

    def copy_of(source, target, index, to):
        return pltpu.make_async_remote_copy(
            src_ref=source,
            dst_ref=buf.at[target],
            send_sem=send_sem.at[index],
            recv_sem=recv_sem.at[target],
            device_id=to,
            device_id_type=MESH,
        )

    def send(variant, source, target, to):
        copy_of(source, target, sent[variant], to).start()
        sent[variant] += 1

    def arrive(target):
        copy_of(buf.at[target], target, 0, sibling).wait_recv()

    def each_variant(phase):
        for variant in variants:
            here = (core == variant[0]) & (odd == variant[1])
            pl.when(here)(functools.partial(phase, variant))

    sides = ((0, bank), (1, other))

    def first(variant):
        core, odd = variant
        if odd:
            for r in range(2):
                target = slot(4, 0) if core == 1 else STAGE
                send(variant, mine.at[r], target, device(2, r, bank))
        elif core == 1:
            for r in range(2):
                send(variant, mine.at[r], slot(4, 0), device(2, r, bank))
        send(variant, mine.at[1 - core], slot(core, 0), device(0, 1 - core, bank))
        for r in range(2):
            send(variant, mine.at[r], slot(core, 1), device(0, r, other))
        if not odd:
            for r in range(2):
                for at, side in sides:
                    send(variant, mine.at[r], slot(2 + core, at), device(1, r, side))

    def pass_on(variant):
        core, odd = variant
        if odd:
            for block, at in ((3, slot(4, 0)), (2, STAGE)):
                arrive(at)
                for to, side in sides:
                    send(variant, buf.at[at], slot(block, to), device(-1, core, side))
        arrive(slot(1, 1))
        send(variant, buf.at[slot(1, 1)], slot(4, 1), device(2, core, bank))

    def finish(variant):
        for index in range(sent[variant]):
            copy_of(mine.at[0], 0, index, sibling).wait_send()

    each_variant(first)
    tile_copies = [
        pltpu.make_async_remote_copy(
            src_ref=chosen.at[s],
            dst_ref=landed.at[s],
            send_sem=tile_send.at[s],
            recv_sem=tile_recv.at[s],
            device_id=sibling,
            device_id_type=MESH,
        )
        for s in range(2)
    ]
    for copy in tile_copies:
        copy.start()

    lane = lax.broadcasted_iota(jnp.int32, (1, EDGE), 1)
    is_edge = (lane % HALF) == 0
    is_guest = counts[2 * chip] == 2
    is_first = core == 0

    stats[:, 0] = jnp.full((2, HALF, EDGE), -1e30, F32)
    stats[:, 1:] = jnp.zeros((2, 2, HALF, EDGE), F32)

    for load in loads[2:6]:
        load.wait()
    for copy in tile_copies:
        copy.wait_recv()
    here = [chosen[s].astype(F32) for s in range(2)]
    there = [landed[s].astype(F32) for s in range(2)]
    images = (
        jnp.where(is_first, here[0], there[0]),
        jnp.where(
            is_guest,
            jnp.where(is_first, here[1], there[1]),
            jnp.where(is_first, there[0], here[0]),
        ),
    )
    res, ims = [], []
    for s in range(2):
        image = images[s]
        centred = image - jnp.sum(image) * (1.0 / (EDGE * EDGE))
        power = jnp.sum(centred * centred) * (1.0 / (EDGE * EDGE))
        unit = (centred / jnp.sqrt(power + 1e-5)).astype(BF16)
        passed = dot(unit, rows[0])
        res.append(passed[:, :HALF])
        ims.append(passed[:, HALF:])
        column = lax.dot_general(
            alt_rows[...], unit, (((1,), (1,)), ((), ())), preferred_element_type=F32
        )[:8]
        swapped = jnp.concatenate([column[:, HALF:], column[:, :HALF]], axis=1)
        column = jnp.where(bank == 1, swapped, column)
        spread = jnp.broadcast_to(column[:1], (HALF, EDGE))
        spread = pltpu.roll(spread, HALF + 1, 1, stride=1, stride_axis=0)
        circ[s] = dot(flip_rows[...], spread[:, :SIDE].astype(BF16)).astype(BF16)
    tile_re = jnp.concatenate(res, axis=1).astype(BF16)
    tile_im = jnp.where(is_edge, 0.0, jnp.concatenate(ims, axis=1)).astype(BF16)
    products = dot(tile_cols[...], jnp.concatenate([tile_re, tile_im], axis=0)) * (1.0 / EDGE)
    for s in range(2):
        part = products[:, s * HALF : (s + 1) * HALF].astype(BF16)
        spec[s] = jnp.concatenate([part, part], axis=1)

    for load in loads[6:]:
        load.wait()
    each_variant(pass_on)

    def row_stage(block):
        parts_re, parts_im = [], []
        for at in range(2):
            unit = buf[slot(block, at)]
            right = unit[SIDE:]
            top = dot(jnp.concatenate([unit[:96], right], axis=1), rows[1])
            bottom = dot(jnp.concatenate([unit[96:SIDE], right], axis=1), rows[2])
            passed = jnp.concatenate([top, bottom], axis=0)
            parts_re.append(passed[:, :HALF])
            parts_im.append(passed[:, HALF:])
        row_re = jnp.concatenate(parts_re, axis=1).astype(BF16)
        row_im = jnp.concatenate(parts_im, axis=1)
        edge = jnp.where(is_edge, row_im, 0.0).astype(BF16)
        row_im = jnp.where(is_edge, 0.0, row_im).astype(BF16)
        return jnp.concatenate([row_re, row_im], axis=0), edge

    def spectra(blocks):
        passed = [row_stage(block) for block in blocks]
        return [(dot(proj_cols[...], row).astype(BF16), edge) for row, edge in passed]

    def cross_stage(s, proj):
        proj_re, proj_im = proj[:EDGE].astype(F32), proj[EDGE:].astype(F32)
        tile_re, tile_im = spec[s, :EDGE].astype(F32), spec[s, EDGE:].astype(F32)
        cross_re = (tile_re * proj_re + tile_im * proj_im).astype(BF16)
        cross_im = (tile_im * proj_re - tile_re * proj_im).astype(BF16)
        return jnp.concatenate([cross_re, cross_im], axis=0)

    def correlate(pairs):
        crosses = [cross_stage(s, proj) for s, (proj, _) in pairs]
        inners = [dot(back[...], cross) for cross in crosses]
        extras = [dot(circ[s], edge) for s, (_, edge) in pairs]
        corrs = []
        for inner, extra in zip(inners, extras):
            inner_re = inner[:HALF].astype(BF16)
            inner_im = (inner[HALF:] + extra).astype(BF16)
            stacked = [
                jnp.concatenate([inner_re[:, lanes], inner_im[:, lanes]], axis=1)
                for lanes in (slice(0, HALF), slice(HALF, EDGE))
            ]
            corrs.append(dot(jnp.concatenate(stacked, axis=0), back_rows[...]))
        for (s, _), corr in zip(pairs, corrs):
            one, two = corr[:HALF], corr[HALF:]
            stats[s, 0] = jnp.maximum(stats[s, 0], jnp.maximum(one, two))
            stats[s, 1] = stats[s, 1] + (one + two)
            stats[s, 2] = stats[s, 2] + (one * one + two * two)

    arrive(slot(1 - core, 0))
    arrive(slot(0, 1))
    now, spare = spectra((0, 1))
    correlate([(0, now), (1, now)])
    arrive_edge = spare[1]

    @pl.when(odd == 0)
    def _():
        arrive(slot(4, 0))

    arrive(slot(4, 1))
    (far,) = spectra((4,))
    chosen_far = (
        jnp.where(is_guest, far[0].astype(F32), spare[0].astype(F32)).astype(BF16),
        jnp.where(is_guest, far[1].astype(F32), arrive_edge.astype(F32)).astype(BF16),
    )
    correlate([(0, far), (1, chosen_far)])
    for block in (3, 2):
        for at in range(2):
            arrive(slot(block, at))
    one, two = spectra((3, 2))
    correlate([(0, one), (0, two), (1, one), (1, two)])

    parts[...] = stats[...].astype(BF16)
    meet = pltpu.make_async_remote_copy(
        src_ref=parts,
        dst_ref=taken,
        send_sem=part_send,
        recv_sem=part_recv,
        device_id=sibling,
        device_id_type=MESH,
    )
    meet.start()
    each_variant(finish)
    for copy in tile_copies:
        copy.wait_send()
    meet.wait_recv()
    peaks, scores = [], []
    for s in range(2):
        peak = jnp.maximum(stats[s, 0], taken[s, 0].astype(F32))
        mean = (stats[s, 1] + taken[s, 1].astype(F32)) * (1.0 / 16)
        square = (stats[s, 2] + taken[s, 2].astype(F32)) * (1.0 / 16)
        variance = jnp.maximum(square - mean * mean, 0.3)
        peaks.append(peak)
        scores.append((peak - mean) / jnp.sqrt(variance))
    live = counts[me]
    for out, maps in ((peak_out, peaks), (score_out, scores)):
        out[0] = jnp.where(live > 0, jnp.where(is_first, maps[0], maps[1]), 0.0)
        out[1] = jnp.where(live > 1, maps[1], 0.0)
    meet.wait_send()


def body(tile_pool, tile_list, counts, projections):
    tables = [jnp.asarray(t) for t in make_tables()]
    any_spec = pl.BlockSpec(memory_space=pl.ANY)
    vmem = pl.BlockSpec(memory_space=pltpu.VMEM)
    smem = pl.BlockSpec(memory_space=pltpu.SMEM)
    out = jax.ShapeDtypeStruct((2, HALF, EDGE), F32)
    return pl.pallas_call(
        kernel,
        out_shape=(out, out),
        in_specs=[any_spec, smem, smem] + [any_spec] * 8,
        out_specs=(vmem, vmem),
        scratch_shapes=[
            pltpu.VMEM((4, EDGE, EDGE), BF16),
            pltpu.VMEM((2, SIDE, SIDE), BF16),
            pltpu.VMEM((3, EDGE, EDGE), BF16),
            pltpu.VMEM((2 * EDGE, 2 * EDGE), BF16),
            pltpu.VMEM((2 * EDGE, 2 * SIDE), BF16),
            pltpu.VMEM((EDGE, 2 * EDGE), BF16),
            pltpu.VMEM((EDGE, EDGE), BF16),
            pltpu.VMEM((16, EDGE), BF16),
            pltpu.VMEM((HALF, HALF), BF16),
            pltpu.VMEM((2,) + UNIT, BF16),
            pltpu.VMEM((STAGE + 1,) + UNIT, BF16),
            pltpu.VMEM((2, EDGE, EDGE), BF16),
            pltpu.VMEM((2, EDGE, EDGE), BF16),
            pltpu.VMEM((2, 2 * EDGE, EDGE), BF16),
            pltpu.VMEM((2, HALF, SIDE), BF16),
            pltpu.VMEM((2, 3, HALF, EDGE), F32),
            pltpu.VMEM((2, 3, HALF, EDGE), BF16),
            pltpu.VMEM((2, 3, HALF, EDGE), BF16),
            pltpu.SemaphoreType.DMA((9,)),
            pltpu.SemaphoreType.DMA((20,)),
            pltpu.SemaphoreType.DMA((STAGE + 1,)),
            pltpu.SemaphoreType.DMA((2,)),
            pltpu.SemaphoreType.DMA((2,)),
            pltpu.SemaphoreType.DMA,
            pltpu.SemaphoreType.DMA,
        ],
        compiler_params=pltpu.CompilerParams(
            collective_id=0, has_side_effects=True, vmem_limit_bytes=56 << 20
        ),
    )(tile_pool, tile_list, counts, projections, *tables)


def solution(mesh):
    in_specs = (P("blk", None, None), P("blk"), P(), P(("blk", "bank"), None, None))
    out_specs = (P("blk", "bank", None), P("blk", "bank", None))
    return jax.shard_map(body, mesh=mesh, in_specs=in_specs, out_specs=out_specs, check_vma=False)
```

time: 47.1 us -> 28.8 us (0.61)
  Pallas kernels: 34.9 us -> 25.6 us
  local copies, waits for them, and re-layouts: 11.1 us -> 2.42 us
    pallas_call x1, Pallas kernels: 34.9 us -> 25.6 us  [body(): pl.pallas_call(kernel, out_shape=(out, out), in_specs=[any_spec, smem, sm...]
    unnamed x24 -> x4, local copies, waits for them, and re-layouts: 11.1 us -> 2.42 us
where the time goes in v2:
time: 28.8 us; the launch traced here: 28.7 us
  Pallas kernels  25.6 us (89%)
  local copies, waits for them, and re-layouts  2.42 us (8%)
  between operations  0.65 us (2%)
    pallas_call x1, Pallas kernels, body(): pl.pallas_call(kernel, out_shape=(out, out), in_specs=[any_spec, smem, sm...  25.6 us
    unnamed x4, local copies, waits for them, and re-layouts  2.42 us

profile of v2, /device:TPU:1, one launch (start us, length us, event | category | flops | bytes accessed | tf_op | source)
XLA Modules:
  0.0 28.7 jit_solution(9763272941289511199)
XLA Ops:
  0.6 25.6 %shard_map.122 = (f32[2,128,256]{2,1,0:T(8,128)}, f32[2,128,256]{2,1,0:T(8,128)}) custom-call(bf16[4,256,256]{2,1,0:T(8,128)(2,1)} %pool_in.1, s32[2]{0:T(128)} %tile_list.1, s32[128]{0:T(128)} %counts.1, bf16[2,192,192]{2,1,0:T(8,128)(2,1)} %raw_in.1, bf16[3,256,256]{2,1,0:T(8,128)(2,1)} %constant.14.clone.rows_in, ...), custom_call_target="tpu_custom_call" | custom-call | tf_op jit(solution)/shard_map/pallas_call | solution.py:383
  26.3 0.0 copy-start
  26.3 1.7 %copy.15 = f32[2,128,256]{2,1,0:T(8,128)} copy(f32[2,128,256]{2,1,0:T(8,128)} %get-tuple-element.4) | data formatting | bytes 524288
  28.0 0.0 copy-done
  28.0 0.7 %copy.16 = f32[2,128,256]{2,1,0:T(8,128)} copy(f32[2,128,256]{2,1,0:T(8,128)S(1)} %copy-done) | data formatting | bytes 524288
Async XLA Ops:
  26.3 1.7 %copy-start = (f32[2,128,256]{2,1,0:T(8,128)S(1)}, f32[2,128,256]{2,1,0:T(8,128)}, u32[]{:S(2)}) copy-start(f32[2,128,256]{2,1,0:T(8,128)} %get-tuple-element.5) | copy-start | bytes 786436

commit v3 on v2

--- a/solution.py
+++ b/solution.py
@@ -14,6 +14,7 @@
 HALF = 128
 CHIPS = 64
 UNIT = (288, 128)
+PIECE = 144
 BF16 = jnp.bfloat16
 F32 = jnp.float32
 MESH = pl.DeviceIdType.MESH
@@ -70,16 +71,17 @@
 def kernel(
     pool_in, tile_list, counts, raw_in, rows_in, tile_cols_in, proj_cols_in, back_cols_in,
     back_rows_in, alt_in, flip_in,
-    peak_out, score_out,
+    own_out, taken_out,
     pool, raw, rows, tile_cols, proj_cols, back, back_rows, alt_rows, flip_rows,
-    mine, buf, chosen, landed, spec, circ, stats, parts, taken,
-    load_sem, send_sem, recv_sem, tile_send, tile_recv, part_send, part_recv,
+    mine, buf, chosen, landed, spec, circ, stats, held_proj, held_edge, parts,
+    load_sem, send_sem, recv_sem, half_recv, tile_send, tile_recv, part_send, part_recv,
 ):
     me = lax.axis_index("blk")
     bank = lax.axis_index("bank")
     chip = me // 2
     core = me % 2
     odd = chip % 2
+    first_plane = (chip // 2) % 8 == 0
     other = 1 - bank
 
     def device(ahead, which, side):
@@ -95,8 +97,7 @@
         pltpu.make_async_copy(source, target, load_sem.at[n])
         for n, (source, target) in enumerate(zip(sources, targets))
     ]
-    for load in loads:
-        load.start()
+    loads[0].start()
 
     barrier = pltpu.get_barrier_semaphore()
 
@@ -124,22 +125,19 @@
                 greet(device(-1, which, side))
 
     loads[0].wait()
+    for load in loads[1:]:
+        load.start()
+    packs = []
     for r in range(2):
         image = raw[r].astype(F32)
         centred = image - jnp.sum(image) * (1.0 / (SIDE * SIDE))
         power = jnp.sum(centred * centred) * (1.0 / (SIDE * SIDE))
         unit = centred / (SIDE * jnp.sqrt(power + 1e-5))
         right = jnp.concatenate([unit[:96, HALF:], unit[96:, HALF:]], axis=1)
-        packed = jnp.concatenate([unit[:, :HALF], right], axis=0).astype(BF16)
-        mine[r] = packed
-
-        @pl.when(core == r)
-        def _():
-            buf[slot(r, 0)] = packed
-
-    loads[1].wait()
-    for s in range(2):
-        chosen[s] = pool[tile_list[s]]
+        packs.append(jnp.concatenate([unit[:, :HALF], right], axis=0))
+    for r in range(2):
+        mine[r] = packs[r].astype(BF16)
+    buf[2 * core] = jnp.where(core == 0, packs[0], packs[1]).astype(BF16)
 
     @pl.when(odd == 1)
     def _():
@@ -154,28 +152,37 @@
         pl.semaphore_wait(barrier, 9)
 
     variants = [(which, parity) for which in (0, 1) for parity in (0, 1)]
-    sent = {variant: 0 for variant in variants}
-
-    def copy_of(source, target, index, to):
+    sent = {variant: [] for variant in variants}
+
+    def copy_of(source, target, sent_sem, got_sem, to):
         return pltpu.make_async_remote_copy(
             src_ref=source,
-            dst_ref=buf.at[target],
-            send_sem=send_sem.at[index],
-            recv_sem=recv_sem.at[target],
+            dst_ref=target,
+            send_sem=sent_sem,
+            recv_sem=got_sem,
             device_id=to,
             device_id_type=MESH,
         )
 
     def send(variant, source, target, to):
-        copy_of(source, target, sent[variant], to).start()
-        sent[variant] += 1
+        index = len(sent[variant])
+        sent[variant].append(UNIT[0])
+        copy_of(source, buf.at[target], send_sem.at[index], recv_sem.at[target], to).start()
+
+    def send_piece(variant, source, piece, target, got_sem, to):
+        index = len(sent[variant])
+        sent[variant].append(PIECE)
+        rows_of = pl.ds(piece * PIECE, PIECE)
+        copy_of(
+            source.at[rows_of], buf.at[target, rows_of], send_sem.at[index], got_sem, to
+        ).start()
 
     def arrive(target):
-        copy_of(buf.at[target], target, 0, sibling).wait_recv()
-
-    def each_variant(phase):
+        copy_of(buf.at[target], buf.at[target], send_sem.at[0], recv_sem.at[target], sibling).wait_recv()
+
+    def each_variant(phase, when=True):
         for variant in variants:
-            here = (core == variant[0]) & (odd == variant[1])
+            here = (core == variant[0]) & (odd == variant[1]) & when
             pl.when(here)(functools.partial(phase, variant))
 
     sides = ((0, bank), (1, other))
@@ -183,9 +190,11 @@
     def first(variant):
         core, odd = variant
         if odd:
-            for r in range(2):
-                target = slot(4, 0) if core == 1 else STAGE
-                send(variant, mine.at[r], target, device(2, r, bank))
+            target = slot(4, 0) if core == 1 else STAGE
+            for piece in range(2):
+                for r in range(2):
+                    got = half_recv.at[2 * (1 - core) + piece]
+                    send_piece(variant, mine.at[r], piece, target, got, device(2, r, bank))
         elif core == 1:
             for r in range(2):
                 send(variant, mine.at[r], slot(4, 0), device(2, r, bank))
@@ -197,21 +206,36 @@
                 for at, side in sides:
                     send(variant, mine.at[r], slot(2 + core, at), device(1, r, side))
 
-    def pass_on(variant):
+    def pass_far(variant):
+        core, odd = variant
+        arrive(slot(1, 1))
+        send(variant, buf.at[slot(1, 1)], slot(4, 1), device(2, core, bank))
+
+    def pass_near(variant):
         core, odd = variant
         if odd:
-            for block, at in ((3, slot(4, 0)), (2, STAGE)):
-                arrive(at)
-                for to, side in sides:
-                    send(variant, buf.at[at], slot(block, to), device(-1, core, side))
-        arrive(slot(1, 1))
-        send(variant, buf.at[slot(1, 1)], slot(4, 1), device(2, core, bank))
+            for piece in range(2):
+                for n, (block, at) in enumerate(((3, slot(4, 0)), (2, STAGE))):
+                    rows_of = pl.ds(piece * PIECE, PIECE)
+                    place = buf.at[at, rows_of]
+                    got = half_recv.at[2 * n + piece]
+                    copy_of(place, place, send_sem.at[0], got, sibling).wait_recv()
+                    for to, side in sides:
+                        target = slot(block, to)
+                        send_piece(
+                            variant, buf.at[at], piece, target, recv_sem.at[target],
+                            device(-1, core, side),
+                        )
 
     def finish(variant):
-        for index in range(sent[variant]):
-            copy_of(mine.at[0], 0, index, sibling).wait_send()
+        for index, size in enumerate(sent[variant]):
+            piece = mine.at[0, pl.ds(0, size)]
+            copy_of(piece, piece, send_sem.at[index], recv_sem.at[0], sibling).wait_send()
 
     each_variant(first)
+    loads[1].wait()
+    for s in range(2):
+        chosen[s] = pool[tile_list[s]]
     tile_copies = [
         pltpu.make_async_remote_copy(
             src_ref=chosen.at[s],
@@ -274,7 +298,11 @@
 
     for load in loads[6:]:
         load.wait()
-    each_variant(pass_on)
+    before = {variant: list(sizes) for variant, sizes in sent.items()}
+    each_variant(pass_near, jnp.logical_not(first_plane))
+    each_variant(pass_far)
+    after = dict(sent)
+    sent.update(before)
 
     def row_stage(block):
         parts_re, parts_im = [], []
@@ -326,52 +354,71 @@
     arrive(slot(0, 1))
     now, spare = spectra((0, 1))
     correlate([(0, now), (1, now)])
-    arrive_edge = spare[1]
-
-    @pl.when(odd == 0)
-    def _():
-        arrive(slot(4, 0))
-
-    arrive(slot(4, 1))
-    (far,) = spectra((4,))
-    chosen_far = (
-        jnp.where(is_guest, far[0].astype(F32), spare[0].astype(F32)).astype(BF16),
-        jnp.where(is_guest, far[1].astype(F32), arrive_edge.astype(F32)).astype(BF16),
-    )
-    correlate([(0, far), (1, chosen_far)])
-    for block in (3, 2):
-        for at in range(2):
-            arrive(slot(block, at))
-    one, two = spectra((3, 2))
-    correlate([(0, one), (0, two), (1, one), (1, two)])
-
-    parts[...] = stats[...].astype(BF16)
-    meet = pltpu.make_async_remote_copy(
-        src_ref=parts,
-        dst_ref=taken,
-        send_sem=part_send,
-        recv_sem=part_recv,
-        device_id=sibling,
-        device_id_type=MESH,
-    )
-    meet.start()
+
+    def chip_before():
+        for block in (3, 2):
+            for at in range(2):
+                arrive(slot(block, at))
+        one, two = spectra((3, 2))
+        correlate([(0, one), (0, two), (1, one), (1, two)])
+
+    def two_before():
+        @pl.when(odd == 0)
+        def _():
+            arrive(slot(4, 0))
+
+        arrive(slot(4, 1))
+        (far,) = spectra((4,))
+        guest = [jnp.where(is_guest, f.astype(F32), c.astype(F32)).astype(BF16) for f, c in zip(far, held())]
+        correlate([(0, far), (1, guest)])
+
+    held_proj[...], held_edge[...] = spare
+
+    def held():
+        return held_proj[...], held_edge[...]
+
+    each_variant(pass_near, first_plane)
+    sent.update(after)
+
+    def last_steps(step, carry):
+        pl.when((step == 0) == (odd == 1))(chip_before)
+        pl.when((step == 0) == (odd == 0))(two_before)
+        return carry
+
+    lax.fori_loop(0, 2, last_steps, 0)
+
+    moves = []
+    for s in range(2):
+        parts[s] = stats[s].astype(BF16)
+        moves.append(
+            copy_of(parts.at[s], taken_out.at[s], part_send.at[s], part_recv.at[s], sibling)
+        )
+        moves.append(pltpu.make_async_copy(parts.at[s], own_out.at[s], load_sem.at[s]))
+        moves[-2].start()
+        moves[-1].start()
     each_variant(finish)
     for copy in tile_copies:
         copy.wait_send()
-    meet.wait_recv()
+    for move in moves:
+        move.wait()
+
+
+def merge_kernel(counts, own, taken, peak_out, score_out):
+    me = lax.axis_index("blk")
+    is_first = me % 2 == 0
+    live = counts[me]
     peaks, scores = [], []
     for s in range(2):
-        peak = jnp.maximum(stats[s, 0], taken[s, 0].astype(F32))
-        mean = (stats[s, 1] + taken[s, 1].astype(F32)) * (1.0 / 16)
-        square = (stats[s, 2] + taken[s, 2].astype(F32)) * (1.0 / 16)
+        mine, theirs = own[s].astype(F32), taken[s].astype(F32)
+        peak = jnp.maximum(mine[0], theirs[0])
+        mean = (mine[1] + theirs[1]) * (1.0 / 16)
+        square = (mine[2] + theirs[2]) * (1.0 / 16)
         variance = jnp.maximum(square - mean * mean, 0.3)
         peaks.append(peak)
         scores.append((peak - mean) / jnp.sqrt(variance))
-    live = counts[me]
     for out, maps in ((peak_out, peaks), (score_out, scores)):
         out[0] = jnp.where(live > 0, jnp.where(is_first, maps[0], maps[1]), 0.0)
         out[1] = jnp.where(live > 1, maps[1], 0.0)
-    meet.wait_send()
 
 
 def body(tile_pool, tile_list, counts, projections):
@@ -379,12 +426,14 @@
     any_spec = pl.BlockSpec(memory_space=pl.ANY)
     vmem = pl.BlockSpec(memory_space=pltpu.VMEM)
     smem = pl.BlockSpec(memory_space=pltpu.SMEM)
-    out = jax.ShapeDtypeStruct((2, HALF, EDGE), F32)
-    return pl.pallas_call(
+    own, taken = pl.pallas_call(
         kernel,
-        out_shape=(out, out),
+        out_shape=(
+            jax.ShapeDtypeStruct((2, 3, HALF, EDGE), BF16),
+            jax.ShapeDtypeStruct((2, 3, HALF, EDGE), BF16),
+        ),
         in_specs=[any_spec, smem, smem] + [any_spec] * 8,
-        out_specs=(vmem, vmem),
+        out_specs=(any_spec, any_spec),
         scratch_shapes=[
             pltpu.VMEM((4, EDGE, EDGE), BF16),
             pltpu.VMEM((2, SIDE, SIDE), BF16),
@@ -402,20 +451,32 @@
             pltpu.VMEM((2, 2 * EDGE, EDGE), BF16),
             pltpu.VMEM((2, HALF, SIDE), BF16),
             pltpu.VMEM((2, 3, HALF, EDGE), F32),
-            pltpu.VMEM((2, 3, HALF, EDGE), BF16),
+            pltpu.VMEM((2 * EDGE, EDGE), BF16),
+            pltpu.VMEM((SIDE, EDGE), BF16),
             pltpu.VMEM((2, 3, HALF, EDGE), BF16),
             pltpu.SemaphoreType.DMA((9,)),
             pltpu.SemaphoreType.DMA((20,)),
             pltpu.SemaphoreType.DMA((STAGE + 1,)),
+            pltpu.SemaphoreType.DMA((4,)),
             pltpu.SemaphoreType.DMA((2,)),
             pltpu.SemaphoreType.DMA((2,)),
-            pltpu.SemaphoreType.DMA,
-            pltpu.SemaphoreType.DMA,
+            pltpu.SemaphoreType.DMA((2,)),
+            pltpu.SemaphoreType.DMA((2,)),
         ],
         compiler_params=pltpu.CompilerParams(
             collective_id=0, has_side_effects=True, vmem_limit_bytes=56 << 20
         ),
     )(tile_pool, tile_list, counts, projections, *tables)
+    out = jax.ShapeDtypeStruct((2, HALF, EDGE), F32)
+    part = pl.BlockSpec((2, 3, HALF // 2, EDGE), lambda i: (0, 0, i, 0))
+    out_part = pl.BlockSpec((2, HALF // 2, EDGE), lambda i: (0, i, 0))
+    return pl.pallas_call(
+        merge_kernel,
+        grid=(2,),
+        out_shape=(out, out),
+        in_specs=[smem, part, part],
+        out_specs=(out_part, out_part),
+    )(counts, own, taken)
 
 
 def solution(mesh):

time: 28.8 us -> 27.4 us (0.951)
  local copies, waits for them, and re-layouts: 2.42 us -> 0 us
  Pallas kernels: 25.6 us -> 26.6 us
    unnamed x4 -> x0, local copies, waits for them, and re-layouts: 2.42 us -> none
    pallas_call x1 -> x2, Pallas kernels: 25.6 us -> 26.6 us  [the longest x1 24.5 us: body(): pl.pallas_call(kernel, out_shape=(jax.ShapeDtypeStruct((2, 3, HALF, EDGE)...]
where the time goes in v3:
time: 27.4 us; the launch traced here: 27.2 us
  Pallas kernels  26.6 us (97%)
  between operations  0.64 us (2%)
    pallas_call x1, Pallas kernels, body(): pl.pallas_call(kernel, out_shape=(jax.ShapeDtypeStruct((2, 3, HALF, EDGE)...  24.5 us
    pallas_call x1, Pallas kernels, body(): pl.pallas_call(merge_kernel, grid=(2,), out_shape=(out, out), in_specs=[s...  2.09 us

profile of v3, /device:TPU:1, one launch (start us, length us, event | category | flops | bytes accessed | tf_op | source)
XLA Modules:
  0.0 27.2 jit_solution(1739247619254120162)
XLA Ops:
  0.6 24.5 %shard_map.122 = (bf16[2,3,128,256]{3,2,1,0:T(8,128)(2,1)}, bf16[2,3,128,256]{3,2,1,0:T(8,128)(2,1)}) custom-call(bf16[4,256,256]{2,1,0:T(8,128)(2,1)} %pool_in.1, s32[2]{0:T(128)} %tile_list.1, s32[128]{0:T(128)} %counts.3, bf16[2,192,192]{2,1,0:T(8,128)(2,1)} %raw_in.1, bf16[3,256,256]{2,1,0:T(8,128)(2,1)} %constant.14.clone.rows_in, ...), custom_call_target="tpu_custom_call" | custom-call | tf_op jit(solution)/shard_map/pallas_call | solution.py:429
  25.1 2.1 %shard_map.123 = (f32[2,128,256]{2,1,0:T(8,128)}, f32[2,128,256]{2,1,0:T(8,128)}) custom-call(s32[128]{0:T(128)} %counts.3, bf16[2,3,128,256]{3,2,1,0:T(8,128)(2,1)} %get-tuple-element.4.own, bf16[2,3,128,256]{3,2,1,0:T(8,128)(2,1)} %get-tuple-element.5.taken), custom_call_target="tpu_custom_call" | custom-call | tf_op jit(solution)/shard_map/pallas_call | solution.py:473

commit v4 on v3

--- a/solution.py
+++ b/solution.py
@@ -64,6 +64,11 @@
     return tuple(cast(t) for t in (rows, tile_cols, proj_cols, back_cols, back_rows, alt_rows, flip_rows))
 
 
+def total_of(field):
+    lines = jnp.sum(field, axis=0, keepdims=True)
+    return jnp.sum(lines, axis=1, keepdims=True)
+
+
 def dot(a, b):
     return jnp.dot(a, b, preferred_element_type=F32)
 
@@ -108,18 +113,16 @@
     greet(device(0, 0, other))
     greet(device(0, 1, other))
     greet(device(-2, 1, bank))
+    greet(device(-2, 1, other))
 
     @pl.when(odd == 0)
     def _():
         greet(device(1, core, bank))
         greet(device(1, core, other))
 
-    @pl.when((odd == 1) | (core == 0))
+    @pl.when(odd == 1)
     def _():
         greet(device(-2, 0, bank))
-
-    @pl.when(odd == 1)
-    def _():
         for side in (bank, other):
             for which in (0, 1):
                 greet(device(-1, which, side))
@@ -130,26 +133,26 @@
     packs = []
     for r in range(2):
         image = raw[r].astype(F32)
-        centred = image - jnp.sum(image) * (1.0 / (SIDE * SIDE))
-        power = jnp.sum(centred * centred) * (1.0 / (SIDE * SIDE))
-        unit = centred / (SIDE * jnp.sqrt(power + 1e-5))
+        centred = image - total_of(image) * (1.0 / (SIDE * SIDE))
+        power = total_of(centred * centred) * (1.0 / (SIDE * SIDE))
+        unit = centred * (1.0 / (SIDE * jnp.sqrt(power + 1e-5)))
         right = jnp.concatenate([unit[:96, HALF:], unit[96:, HALF:]], axis=1)
         packs.append(jnp.concatenate([unit[:, :HALF], right], axis=0))
     for r in range(2):
         mine[r] = packs[r].astype(BF16)
     buf[2 * core] = jnp.where(core == 0, packs[0], packs[1]).astype(BF16)
 
-    @pl.when(odd == 1)
+    @pl.when(core == 0)
     def _():
         pl.semaphore_wait(barrier, 7)
 
-    @pl.when((odd == 0) & (core == 0))
-    def _():
-        pl.semaphore_wait(barrier, 8)
+    @pl.when((odd == 1) & (core == 1))
+    def _():
+        pl.semaphore_wait(barrier, 9)
 
     @pl.when((odd == 0) & (core == 1))
     def _():
-        pl.semaphore_wait(barrier, 9)
+        pl.semaphore_wait(barrier, 11)
 
     variants = [(which, parity) for which in (0, 1) for parity in (0, 1)]
     sent = {variant: [] for variant in variants}
@@ -198,6 +201,9 @@
         elif core == 1:
             for r in range(2):
                 send(variant, mine.at[r], slot(4, 0), device(2, r, bank))
+        if core == 1:
+            for r in range(2):
+                send(variant, mine.at[r], slot(4, 1), device(2, r, other))
         send(variant, mine.at[1 - core], slot(core, 0), device(0, 1 - core, bank))
         for r in range(2):
             send(variant, mine.at[r], slot(core, 1), device(0, r, other))
@@ -205,11 +211,6 @@
             for r in range(2):
                 for at, side in sides:
                     send(variant, mine.at[r], slot(2 + core, at), device(1, r, side))
-
-    def pass_far(variant):
-        core, odd = variant
-        arrive(slot(1, 1))
-        send(variant, buf.at[slot(1, 1)], slot(4, 1), device(2, core, bank))
 
     def pass_near(variant):
         core, odd = variant
@@ -275,9 +276,9 @@
     res, ims = [], []
     for s in range(2):
         image = images[s]
-        centred = image - jnp.sum(image) * (1.0 / (EDGE * EDGE))
-        power = jnp.sum(centred * centred) * (1.0 / (EDGE * EDGE))
-        unit = (centred / jnp.sqrt(power + 1e-5)).astype(BF16)
+        centred = image - total_of(image) * (1.0 / (EDGE * EDGE))
+        power = total_of(centred * centred) * (1.0 / (EDGE * EDGE))
+        unit = (centred * (1.0 / jnp.sqrt(power + 1e-5))).astype(BF16)
         passed = dot(unit, rows[0])
         res.append(passed[:, :HALF])
         ims.append(passed[:, HALF:])
@@ -300,29 +301,29 @@
         load.wait()
     before = {variant: list(sizes) for variant, sizes in sent.items()}
     each_variant(pass_near, jnp.logical_not(first_plane))
-    each_variant(pass_far)
     after = dict(sent)
     sent.update(before)
 
-    def row_stage(block):
-        parts_re, parts_im = [], []
-        for at in range(2):
-            unit = buf[slot(block, at)]
-            right = unit[SIDE:]
-            top = dot(jnp.concatenate([unit[:96], right], axis=1), rows[1])
-            bottom = dot(jnp.concatenate([unit[96:SIDE], right], axis=1), rows[2])
-            passed = jnp.concatenate([top, bottom], axis=0)
-            parts_re.append(passed[:, :HALF])
-            parts_im.append(passed[:, HALF:])
-        row_re = jnp.concatenate(parts_re, axis=1).astype(BF16)
-        row_im = jnp.concatenate(parts_im, axis=1)
-        edge = jnp.where(is_edge, row_im, 0.0).astype(BF16)
-        row_im = jnp.where(is_edge, 0.0, row_im).astype(BF16)
-        return jnp.concatenate([row_re, row_im], axis=0), edge
-
     def spectra(blocks):
-        passed = [row_stage(block) for block in blocks]
-        return [(dot(proj_cols[...], row).astype(BF16), edge) for row, edge in passed]
+        units = [buf[slot(block, at)] for block in blocks for at in range(2)]
+        tops = [jnp.concatenate([unit[:96], unit[SIDE:]], axis=1) for unit in units]
+        bottoms = [jnp.concatenate([unit[96:SIDE], unit[SIDE:]], axis=1) for unit in units]
+        top = dot(jnp.concatenate(tops, axis=0), rows[1])
+        bottom = dot(jnp.concatenate(bottoms, axis=0), rows[2])
+        out = []
+        for n in range(len(blocks)):
+            parts_re, parts_im = [], []
+            for at in range(2):
+                lines = slice((2 * n + at) * 96, (2 * n + at + 1) * 96)
+                passed = jnp.concatenate([top[lines], bottom[lines]], axis=0)
+                parts_re.append(passed[:, :HALF])
+                parts_im.append(passed[:, HALF:])
+            row_re = jnp.concatenate(parts_re, axis=1).astype(BF16)
+            row_im = jnp.concatenate(parts_im, axis=1)
+            edge = jnp.where(is_edge, row_im, 0.0).astype(BF16)
+            row_im = jnp.where(is_edge, 0.0, row_im).astype(BF16)
+            out.append((jnp.concatenate([row_re, row_im], axis=0), edge))
+        return [(dot(proj_cols[...], row).astype(BF16), edge) for row, edge in out]
 
     def cross_stage(s, proj):
         proj_re, proj_im = proj[:EDGE].astype(F32), proj[EDGE:].astype(F32)
@@ -352,6 +353,7 @@
 
     arrive(slot(1 - core, 0))
     arrive(slot(0, 1))
+    arrive(slot(1, 1))
     now, spare = spectra((0, 1))
     correlate([(0, now), (1, now)])
 
@@ -387,20 +389,38 @@
 
     lax.fori_loop(0, 2, last_steps, 0)
 
-    moves = []
-    for s in range(2):
-        parts[s] = stats[s].astype(BF16)
-        moves.append(
-            copy_of(parts.at[s], taken_out.at[s], part_send.at[s], part_recv.at[s], sibling)
-        )
-        moves.append(pltpu.make_async_copy(parts.at[s], own_out.at[s], load_sem.at[s]))
-        moves[-2].start()
-        moves[-1].start()
+    theirs = [
+        copy_of(parts.at[s], taken_out.at[s], part_send.at[s], part_recv.at[s], sibling)
+        for s in range(2)
+    ]
+    ours = [pltpu.make_async_copy(parts.at[s], own_out.at[s], load_sem.at[s]) for s in range(2)]
+    parts[1] = stats[1].astype(BF16)
+    theirs[1].start()
+    parts[0] = stats[0].astype(BF16)
+
+    @pl.when(core == 1)
+    def _():
+        theirs[0].start()
+
+    @pl.when(core == 0)
+    def _():
+        ours[0].start()
+
+    ours[1].start()
     each_variant(finish)
     for copy in tile_copies:
         copy.wait_send()
-    for move in moves:
-        move.wait()
+    theirs[1].wait()
+    ours[1].wait()
+
+    @pl.when(core == 1)
+    def _():
+        theirs[0].wait_send()
+
+    @pl.when(core == 0)
+    def _():
+        theirs[0].wait_recv()
+        ours[0].wait()
 
 
 def merge_kernel(counts, own, taken, peak_out, score_out):

time: 27.4 us -> 26.9 us (0.982)
  Pallas kernels: 26.6 us -> 26.1 us
    pallas_call x1, Pallas kernels: 24.5 us -> 24 us  [body(): pl.pallas_call(kernel, out_shape=(jax.ShapeDtypeStruct((2, 3, HALF, EDGE)...]
where the time goes in v4:
time: 26.9 us; the launch traced here: 26.7 us
  Pallas kernels  26.1 us (97%)
  between operations  0.64 us (2%)
    pallas_call x1, Pallas kernels, body(): pl.pallas_call(kernel, out_shape=(jax.ShapeDtypeStruct((2, 3, HALF, EDGE)...  24 us
    pallas_call x1, Pallas kernels, body(): pl.pallas_call(merge_kernel, grid=(2,), out_shape=(out, out), in_specs=[s...  2.09 us

profile of v4, /device:TPU:1, one launch (start us, length us, event | category | flops | bytes accessed | tf_op | source)
XLA Modules:
  0.0 26.7 jit_solution(7579047024894700326)
XLA Ops:
  0.6 24.0 %shard_map.122 = (bf16[2,3,128,256]{3,2,1,0:T(8,128)(2,1)}, bf16[2,3,128,256]{3,2,1,0:T(8,128)(2,1)}) custom-call(bf16[4,256,256]{2,1,0:T(8,128)(2,1)} %pool_in.1, s32[2]{0:T(128)} %tile_list.1, s32[128]{0:T(128)} %counts.3, bf16[2,192,192]{2,1,0:T(8,128)(2,1)} %raw_in.1, bf16[3,256,256]{2,1,0:T(8,128)(2,1)} %constant.14.clone.rows_in, ...), custom_call_target="tpu_custom_call" | custom-call | tf_op jit(solution)/shard_map/pallas_call | solution.py:449
  24.6 2.1 %shard_map.123 = (f32[2,128,256]{2,1,0:T(8,128)}, f32[2,128,256]{2,1,0:T(8,128)}) custom-call(s32[128]{0:T(128)} %counts.3, bf16[2,3,128,256]{3,2,1,0:T(8,128)(2,1)} %get-tuple-element.4.own, bf16[2,3,128,256]{3,2,1,0:T(8,128)(2,1)} %get-tuple-element.5.taken), custom_call_target="tpu_custom_call" | custom-call | tf_op jit(solution)/shard_map/pallas_call | solution.py:493

commit v5 on v4

--- a/solution.py
+++ b/solution.py
@@ -14,7 +14,8 @@
 HALF = 128
 CHIPS = 64
 UNIT = (288, 128)
-PIECE = 144
+PIECES = 3
+PIECE = UNIT[0] // PIECES
 BF16 = jnp.bfloat16
 F32 = jnp.float32
 MESH = pl.DeviceIdType.MESH
@@ -109,23 +110,26 @@
     def greet(target):
         pl.semaphore_signal(barrier, inc=1, device_id=target, device_id_type=MESH)
 
-    greet(sibling)
+    @pl.when(odd == 0)
+    def _():
+        greet(device(1, core, bank))
+        greet(device(1, core, other))
+
+    @pl.when(odd == 1)
+    def _():
+        for which in (0, 1):
+            for side in (bank, other):
+                greet(device(-1, which, side))
+
     greet(device(0, 0, other))
     greet(device(0, 1, other))
+    greet(sibling)
     greet(device(-2, 1, bank))
     greet(device(-2, 1, other))
 
-    @pl.when(odd == 0)
-    def _():
-        greet(device(1, core, bank))
-        greet(device(1, core, other))
-
     @pl.when(odd == 1)
     def _():
         greet(device(-2, 0, bank))
-        for side in (bank, other):
-            for which in (0, 1):
-                greet(device(-1, which, side))
 
     loads[0].wait()
     for load in loads[1:]:
@@ -194,9 +198,9 @@
         core, odd = variant
         if odd:
             target = slot(4, 0) if core == 1 else STAGE
-            for piece in range(2):
+            for piece in range(PIECES):
                 for r in range(2):
-                    got = half_recv.at[2 * (1 - core) + piece]
+                    got = half_recv.at[PIECES * (1 - core) + piece]
                     send_piece(variant, mine.at[r], piece, target, got, device(2, r, bank))
         elif core == 1:
             for r in range(2):
@@ -215,11 +219,11 @@
     def pass_near(variant):
         core, odd = variant
         if odd:
-            for piece in range(2):
+            for piece in range(PIECES):
                 for n, (block, at) in enumerate(((3, slot(4, 0)), (2, STAGE))):
                     rows_of = pl.ds(piece * PIECE, PIECE)
                     place = buf.at[at, rows_of]
-                    got = half_recv.at[2 * n + piece]
+                    got = half_recv.at[PIECES * n + piece]
                     copy_of(place, place, send_sem.at[0], got, sibling).wait_recv()
                     for to, side in sides:
                         target = slot(block, to)
@@ -362,7 +366,7 @@
             for at in range(2):
                 arrive(slot(block, at))
         one, two = spectra((3, 2))
-        correlate([(0, one), (0, two), (1, one), (1, two)])
+        correlate([(1, one), (1, two), (0, one), (0, two)])
 
     def two_before():
         @pl.when(odd == 0)
@@ -475,9 +479,9 @@
             pltpu.VMEM((SIDE, EDGE), BF16),
             pltpu.VMEM((2, 3, HALF, EDGE), BF16),
             pltpu.SemaphoreType.DMA((9,)),
-            pltpu.SemaphoreType.DMA((20,)),
+            pltpu.SemaphoreType.DMA((32,)),
             pltpu.SemaphoreType.DMA((STAGE + 1,)),
-            pltpu.SemaphoreType.DMA((4,)),
+            pltpu.SemaphoreType.DMA((2 * PIECES,)),
             pltpu.SemaphoreType.DMA((2,)),
             pltpu.SemaphoreType.DMA((2,)),
             pltpu.SemaphoreType.DMA((2,)),

time: 26.9 us -> 26.8 us (level)
  no operation moved by 1% of the time
where the time goes in v5:
time: 26.8 us; the launch traced here: 26.6 us
  Pallas kernels  26 us (97%)
  between operations  0.64 us (2%)
    pallas_call x1, Pallas kernels, body(): pl.pallas_call(kernel, out_shape=(jax.ShapeDtypeStruct((2, 3, HALF, EDGE)...  23.9 us
    pallas_call x1, Pallas kernels, body(): pl.pallas_call(merge_kernel, grid=(2,), out_shape=(out, out), in_specs=[s...  2.09 us

profile of v5, /device:TPU:1, one launch (start us, length us, event | category | flops | bytes accessed | tf_op | source)
XLA Modules:
  0.0 26.6 jit_solution(17425135027874712947)
XLA Ops:
  0.6 23.9 %shard_map.122 = (bf16[2,3,128,256]{3,2,1,0:T(8,128)(2,1)}, bf16[2,3,128,256]{3,2,1,0:T(8,128)(2,1)}) custom-call(bf16[4,256,256]{2,1,0:T(8,128)(2,1)} %pool_in.1, s32[2]{0:T(128)} %tile_list.1, s32[128]{0:T(128)} %counts.3, bf16[2,192,192]{2,1,0:T(8,128)(2,1)} %raw_in.1, bf16[3,256,256]{2,1,0:T(8,128)(2,1)} %constant.14.clone.rows_in, ...), custom_call_target="tpu_custom_call" | custom-call | tf_op jit(solution)/shard_map/pallas_call | solution.py:453
  24.5 2.1 %shard_map.123 = (f32[2,128,256]{2,1,0:T(8,128)}, f32[2,128,256]{2,1,0:T(8,128)}) custom-call(s32[128]{0:T(128)} %counts.3, bf16[2,3,128,256]{3,2,1,0:T(8,128)(2,1)} %get-tuple-element.4.own, bf16[2,3,128,256]{3,2,1,0:T(8,128)(2,1)} %get-tuple-element.5.taken), custom_call_target="tpu_custom_call" | custom-call | tf_op jit(solution)/shard_map/pallas_call | solution.py:497

commit v6 on v5

--- a/solution.py
+++ b/solution.py
@@ -366,7 +366,8 @@
             for at in range(2):
                 arrive(slot(block, at))
         one, two = spectra((3, 2))
-        correlate([(1, one), (1, two), (0, one), (0, two)])
+        correlate([(1, one), (1, two)])
+        correlate([(0, one), (0, two)])
 
     def two_before():
         @pl.when(odd == 0)
@@ -439,7 +440,7 @@
         square = (mine[2] + theirs[2]) * (1.0 / 16)
         variance = jnp.maximum(square - mean * mean, 0.3)
         peaks.append(peak)
-        scores.append((peak - mean) / jnp.sqrt(variance))
+        scores.append((peak - mean) * lax.rsqrt(variance))
     for out, maps in ((peak_out, peaks), (score_out, scores)):
         out[0] = jnp.where(live > 0, jnp.where(is_first, maps[0], maps[1]), 0.0)
         out[1] = jnp.where(live > 1, maps[1], 0.0)

time: 26.8 us -> 26.9 us (level)
  no operation moved by 1% of the time
where the time goes in v6:
time: 26.9 us; the launch traced here: 26.7 us
  Pallas kernels  26.1 us (97%)
  between operations  0.64 us (2%)
    pallas_call x1, Pallas kernels, body(): pl.pallas_call(kernel, out_shape=(jax.ShapeDtypeStruct((2, 3, HALF, EDGE)...  24 us
    pallas_call x1, Pallas kernels, body(): pl.pallas_call(merge_kernel, grid=(2,), out_shape=(out, out), in_specs=[s...  2.05 us

profile of v6, /device:TPU:1, one launch (start us, length us, event | category | flops | bytes accessed | tf_op | source)
XLA Modules:
  0.0 26.7 jit_solution(5797987409915749113)
XLA Ops:
  0.6 24.0 %shard_map.122 = (bf16[2,3,128,256]{3,2,1,0:T(8,128)(2,1)}, bf16[2,3,128,256]{3,2,1,0:T(8,128)(2,1)}) custom-call(bf16[4,256,256]{2,1,0:T(8,128)(2,1)} %pool_in.1, s32[2]{0:T(128)} %tile_list.1, s32[128]{0:T(128)} %counts.3, bf16[2,192,192]{2,1,0:T(8,128)(2,1)} %raw_in.1, bf16[3,256,256]{2,1,0:T(8,128)(2,1)} %constant.14.clone.rows_in, ...), custom_call_target="tpu_custom_call" | custom-call | tf_op jit(solution)/shard_map/pallas_call | solution.py:454
  24.7 2.1 %shard_map.123 = (f32[2,128,256]{2,1,0:T(8,128)}, f32[2,128,256]{2,1,0:T(8,128)}) custom-call(s32[128]{0:T(128)} %counts.3, bf16[2,3,128,256]{3,2,1,0:T(8,128)(2,1)} %get-tuple-element.4.own, bf16[2,3,128,256]{3,2,1,0:T(8,128)(2,1)} %get-tuple-element.5.taken), custom_call_target="tpu_custom_call" | custom-call | tf_op jit(solution)/shard_map/pallas_call | solution.py:498
